TPU v7x, 32 devices: a whole 2x2x4 slice. The times are simulated.
32 devices in a mesh: seq: 8 (over y, x, core), head: 4 (over z).
Axes of the slice: x: 2, y: 2, z: 4, core: 2. Of those that a mesh axis runs over, the one named last changes fastest.
Arguments:
- byte_states: bfloat16 [4, 1024, 1024], P('head', 'seq'), may hold values from -6 to 6
- log_decay: float32 [4, 1024, 32], P('head', 'seq'), may hold values from -2.5 to 0
- group_starts: int32 [4, 192], P('head'), may hold values from 0 to 1023, as said below
- in_weight: bfloat16 [1024, 4352], P('head'), may hold values from -0.1875 to 0.1875
- conv_weight: float32 [4, 2304], replicated, may hold values from -2.5 to 2.5
- norm_gain: float32 [2048], replicated, may hold values from 0.1 to 1.9
- out_weight: bfloat16 [2048, 1024], P('head'), may hold values from -0.125 to 0.125
- qkv_weight: bfloat16 [1024, 3, 4, 128], P(None, None, 'head'), may hold values from -1.5 to 1.5
Outputs:
- encoded: bfloat16 [4, 1024, 1024], P('head', 'seq')
- attended: bfloat16 [4, 192, 4, 128], P(None, 'seq', 'head')
Inputs may be any that keep to these rules, and one draw needn't show every extreme that they name: `group_starts`: strictly increasing, the first entry 0; every group k has all its bytes on the indices k // 24 - 1 to k // 24 + 1 of seq, each index holding 128 consecutive bytes; between 12 and 36 groups begin within the bytes of one index of seq.
All inputs are finite; a program needn't handle non-finite values.
Results may differ from a plain program's by a relative error of at most 0.0095.
Values may be sent and summed in bfloat16 or wider, within the bound.
A program may use at most 128 MiB of HBM per device.

v0:
```python
import math

import jax
import jax.numpy as jnp
from jax import lax
from jax.sharding import PartitionSpec as P

BLOCK = 128


highest = lax.Precision.HIGHEST


def passed_along(value, axis, steps):
    count = lax.axis_size(axis)
    first, last = (max(0, -steps), min(count, count - steps))
    return lax.ppermute(value, axis, [(source, source + steps) for source in range(first, last)])


def entering(x, axis, combine, identity):
    length, place = (lax.axis_size(axis), lax.axis_index(axis))
    everything = jax.tree.map(
        lambda part, kind: lax.all_gather(part.astype(kind), axis), x, (jnp.bfloat16, jnp.bfloat16)
    )
    start = jax.tree.map(
        lambda part, zero: jnp.broadcast_to(jnp.asarray(zero, part.dtype), part.shape), x, identity
    )

    def lap(k, before):
        reached = k < place
        new = combine(
            before, jax.tree.map(lambda part, own: part[k].astype(own.dtype), everything, x)
        )
        return jax.tree.map(lambda a, b: jnp.where(reached, a, b), new, before)

    return lax.fori_loop(0, length, lap, start)


def state_block(hidden_state, block_items):
    head_inputs, write_vectors, read_vectors, decays = block_items
    cumulative = jnp.cumsum(decays, axis=0)
    length = decays.shape[0]
    later_index = lax.broadcasted_iota(jnp.int32, (length, length), 0)
    earlier_index = lax.broadcasted_iota(jnp.int32, (length, length), 1)
    causal = (earlier_index <= later_index)[None]
    spread = cumulative.T[:, :, None] - cumulative.T[:, None, :]
    factor = jnp.where(causal, jnp.exp(jnp.where(causal, spread, 0.0)), 0.0)
    gram_matrix = jnp.dot(read_vectors, write_vectors.T, preferred_element_type=jnp.float32)
    mixed_gram = (factor * gram_matrix[None]).astype(jnp.bfloat16)
    output = jnp.einsum("hts,shp->thp", mixed_gram, head_inputs, preferred_element_type=jnp.float32)
    float_reads = read_vectors.astype(jnp.float32)
    output = output + jnp.exp(cumulative)[:, :, None] * jnp.einsum(
        "tn,hpn->thp", float_reads, hidden_state, precision=highest
    )
    final_log = cumulative[-1]
    tail_decay = jnp.exp(final_log[None, :] - cumulative)
    weighted = (head_inputs.astype(jnp.float32) * tail_decay[:, :, None]).astype(jnp.bfloat16)
    fresh_part = jnp.einsum(
        "shp,sn->hpn", weighted, write_vectors, preferred_element_type=jnp.float32
    )
    hidden_state = jnp.exp(final_log)[:, None, None] * hidden_state + fresh_part
    return (hidden_state, output)


def convolve(padded, conv_weight, length):
    summed = jnp.zeros((length, padded.shape[1]), jnp.float32)
    for offset in range(conv_weight.shape[0]):
        summed = summed + conv_weight[offset] * padded[offset : offset + length].astype(jnp.float32)
    return jax.nn.silu(summed).astype(jnp.bfloat16)


def combine_states(earlier, later):
    return (earlier[0] + later[0], jnp.exp(later[0])[:, None, None] * earlier[1] + later[1])


def local(
    byte_states, log_decay, group_starts, in_weight, conv_weight, norm_gain, out_weight, qkv_weight
):
    states = byte_states[0]
    decays = log_decay[0]
    starts = group_starts[0]
    row_count = states.shape[0]
    model_width = states.shape[1]
    head_count = decays.shape[1]
    inner_width = norm_gain.shape[0]
    head_dim = inner_width // head_count
    state_width = (in_weight.shape[1] - 2 * inner_width) // 2
    float_states = states.astype(jnp.float32)
    normed = (
        float_states
        * lax.rsqrt(jnp.mean(float_states * float_states, axis=-1, keepdims=True) + 1e-05)
    ).astype(jnp.bfloat16)
    columns = normed
    projected = jnp.dot(
        columns,
        lax.all_gather(in_weight, "head", axis=0, tiled=True),
        preferred_element_type=jnp.float32,
    )
    projected = projected.astype(jnp.bfloat16)
    gate_part = projected[:, :inner_width]
    mixer_in = projected[:, inner_width:]
    tap_count = conv_weight.shape[0]
    left_rim = passed_along(mixer_in[row_count - (tap_count - 1) :], "seq", 1)
    padded = jnp.concatenate([left_rim, mixer_in], axis=0)
    convolved = convolve(padded, conv_weight, row_count)
    head_inputs = convolved[:, :inner_width].reshape(row_count, head_count, head_dim)
    write_vectors = convolved[:, inner_width : inner_width + state_width]
    read_vectors = convolved[:, inner_width + state_width :]
    block_rows = BLOCK
    block_count = row_count // block_rows
    start_state = jnp.zeros((head_count, head_dim, state_width), jnp.float32)
    block_items = (
        head_inputs.reshape(block_count, block_rows, head_count, head_dim),
        write_vectors.reshape(block_count, block_rows, state_width),
        read_vectors.reshape(block_count, block_rows, state_width),
        decays.reshape(block_count, block_rows, head_count),
    )
    local_state, outputs = lax.scan(state_block, start_state, block_items)
    outputs = outputs.reshape(row_count, head_count, head_dim)
    cumulative = jnp.cumsum(decays, axis=0)
    identity = (jnp.zeros((head_count,), jnp.float32), jnp.zeros_like(local_state))
    carried = entering((cumulative[-1], local_state), "seq", combine_states, identity)
    outputs = outputs + jnp.exp(cumulative)[:, :, None] * jnp.einsum(
        "tn,hpn->thp", read_vectors.astype(jnp.float32), carried[1], precision=highest
    )
    gated_out = outputs * jax.nn.silu(gate_part.astype(jnp.float32)).reshape(
        row_count, head_count, head_dim
    )
    scaled = (
        gated_out
        * lax.rsqrt(jnp.mean(gated_out * gated_out, axis=-1, keepdims=True) + 1e-05)
        * norm_gain.reshape(head_count, head_dim)
    )
    flat_heads = scaled.reshape(row_count, inner_width).astype(jnp.bfloat16)
    columns = flat_heads
    branch = jnp.dot(
        columns,
        lax.all_gather(out_weight, "head", axis=0, tiled=True),
        preferred_element_type=jnp.float32,
    )
    encoded = (float_states + branch).astype(jnp.bfloat16)
    seq_count = lax.axis_size("seq")
    seq_index = lax.axis_index("seq")
    groups = starts.shape[0]
    per_device = groups // seq_count
    positions = seq_index * row_count + jnp.arange(row_count, dtype=jnp.int32)
    group_id = jnp.sum((starts[None, :] <= positions[:, None]).astype(jnp.int32), axis=1) - 1
    contract_rows = (((0,), (0,)), ((), ()))
    local_id = group_id - (seq_index - 1) * per_device
    onehot = (local_id[:, None] == jnp.arange(3 * per_device, dtype=jnp.int32)[None, :]).astype(
        jnp.bfloat16
    )
    partial_value = lax.dot_general(
        onehot, encoded, contract_rows, preferred_element_type=jnp.float32
    )
    from_above = passed_along(partial_value[:per_device].astype(jnp.bfloat16), "seq", -1).astype(
        jnp.float32
    )
    from_below = passed_along(
        partial_value[2 * per_device :].astype(jnp.bfloat16), "seq", 1
    ).astype(jnp.float32)
    pooled = partial_value[per_device : 2 * per_device] + from_above + from_below
    group_normed = (
        pooled * lax.rsqrt(jnp.mean(pooled * pooled, axis=-1, keepdims=True) + 1e-05)
    ).astype(jnp.bfloat16)
    key_width = qkv_weight.shape[3]
    projection = qkv_weight.reshape(model_width, 3 * key_width)
    triple = jnp.dot(
        lax.all_gather(group_normed, "head", axis=0, tiled=True),
        projection,
        preferred_element_type=jnp.float32,
    ).astype(jnp.bfloat16)
    batch_rows = lax.axis_size("head")
    triple = triple.reshape(batch_rows, per_device, 3, key_width)
    query_rows = triple[:, :, 0]
    key_rows = triple[:, :, 1]
    values = triple[:, :, 2]
    query_pos = seq_index * per_device + jnp.arange(per_device, dtype=jnp.int32)
    row_max = jnp.full((batch_rows, per_device), -1e30, jnp.float32)
    key_fragment = lax.all_gather(key_rows, "seq", axis=1, tiled=True)
    value_piece = lax.all_gather(values, "seq", axis=1, tiled=True)
    key_count = key_fragment.shape[1]
    scores = jnp.einsum(
        "tfv,tuv->tfu", query_rows, key_fragment, preferred_element_type=jnp.float32
    ) / math.sqrt(key_width)
    key_pos = jnp.arange(key_count, dtype=jnp.int32)
    allowed = key_pos[None, None, :] <= query_pos[None, :, None]
    new_max = jnp.maximum(row_max, jnp.max(jnp.where(allowed, scores, -1e30), axis=-1))
    exp_scores = jnp.where(
        allowed, jnp.exp(jnp.where(allowed, scores - new_max[:, :, None], 0.0)), 0.0
    )
    row_total = jnp.sum(exp_scores, axis=-1)
    summed = jnp.einsum(
        "vhf,vfy->vhy",
        exp_scores.astype(jnp.bfloat16),
        value_piece,
        preferred_element_type=jnp.float32,
    )
    row_max, row_total, summed = (new_max, row_total, summed)
    attended = (
        (summed / row_total[:, :, None])
        .astype(jnp.bfloat16)
        .reshape(batch_rows, per_device, 1, key_width)
    )
    return (encoded[None], attended)


def solution(mesh):
    placed = (
        P("head", "seq", None),
        P("head", "seq", None),
        P("head", None),
        P("head", None),
        P(),
        P(),
        P("head", None),
        P(None, None, "head", None),
    )
    return jax.shard_map(
        local,
        mesh=mesh,
        in_specs=placed,
        out_specs=(P("head", "seq", None), P(None, "seq", "head", None)),
        check_vma=False,
    )
```

profile of v0, /device:TPU:0, one launch (start us, length us, event | category | flops | bytes accessed | tf_op | source)
XLA Modules:
  0.0 351.8 jit_solution(14958784745488994262)
XLA Ops:
  8.5 162.1 %all-gather.8.cloned.1.call-done = bf16[1024,4352]{1,0:T(8,128)(2,1)} async-done(((bf16[256,4352]{1,0:T(8,128)(2,1)}), bf16[1024,4352]{1,0:T(8,128)(2,1)}) %all-gather.8.cloned.1.call-update) | async-done | bytes 8912912 | tf_op jit(solution)/shard_map/all_gather | solution.py:96
  170.5 4.9 %convolution_convert_fusion = bf16[128,4352]{1,0:T(8,128)(2,1)S(1)} fusion(bf16[1024,4352]{1,0:T(8,128)(2,1)} %all-gather.8.cloned.1.call-done, bf16[1,128,1024]{2,1,0:T(8,128)(2,1)S(1)} %copy-done, f32[128]{0:T(128)S(1)} %add_rsqrt_fusion.2), kind=kOutput, calls=%fused_computation.3 | convolution fusion | flops 1141800960 | bytes 10289664 | tf_op jit(solution)/shard_map/dot_general | solution.py:94
  175.5 2.0 collective-permute-start
  181.4 11.9 %all-gather.3 = bf16[8,1,32]{2,1,0:T(2,128)(2,1)S(1)} all-gather(bf16[1,1,32]{2,1,0:T(2,128)(2,1)S(1)} %convert_bitcast_fusion), channel_id=1, replica_groups=mesh['seq'=8,'head'=4] {'seq'}, dimensions={0}, use_global_device_ids=true | all-gather | bytes 576 | tf_op jit(solution)/shard_map/all_gather | solution.py:23
  195.1 2.1 convolution_bitcast_fusion
  197.1 1.3 fusion.2
  198.5 19.4 %all-gather.12.cloned.1.call-done = bf16[256,64,128]{2,1,0:T(8,128)(2,1)} async-done(((bf16[32,64,128]{2,1,0:T(8,128)(2,1)}), bf16[256,64,128]{2,1,0:T(8,128)(2,1)}) %all-gather.12.cloned.1.call-update) | async-done | bytes 4194320 | tf_op jit(solution)/shard_map/all_gather | solution.py:23
  217.9 10.8 %while.9 = (s32[]{:T(128)}, f32[32,64,128]{2,1,0:T(8,128)S(1)}, s32[]{:T(128)}, bf16[8,32]{1,0:T(8,128)(2,1)S(1)}, bf16[8,32,64,128]{3,2,1,0:T(8,128)(2,1)}, /*index=5*/s32[]{:T(128)}, s32[]{:T(128)}) while((s32[]{:T(128)}, f32[32,64,128]{2,1,0:T(8,128)S(1)}, s32[]{:T(128)}, bf16[8,32]{1,0:T(8,128)(2,1)S(1)}, ...), condition=%wide.region_3.4_spmd.clone, body=%wide.region_2.3_spmd.clone.sunk | while | flops 1310756 | bytes 2621873 | solution.py:36
  217.9 1.3 fusion.60
  219.2 1.3 fusion.60
  220.5 1.3 fusion.60
  221.9 1.3 fusion.60
  223.2 1.3 fusion.60
  224.6 1.3 fusion.60
  225.9 1.3 fusion.60
  227.3 1.3 fusion.60
  228.7 1.5 multiply_reduce_fusion
  230.5 69.8 %all-gather.10.cloned.1.call-done = bf16[2048,1024]{1,0:T(8,128)(2,1)} async-done(((bf16[512,1024]{1,0:T(8,128)(2,1)}), bf16[2048,1024]{1,0:T(8,128)(2,1)}) %all-gather.10.cloned.1.call-update) | async-done | bytes 4194320 | tf_op jit(solution)/shard_map/all_gather | solution.py:138
  300.2 2.9 fusion.5
  303.5 1.7 collective-permute-start.2
  307.0 2.7 collective-permute-done.1
  309.9 13.8 %all_gather.30 = bf16[96,1024]{1,0:T(8,128)(2,1)S(1)} all-gather(bf16[24,1024]{1,0:T(8,128)(2,1)S(1)} %multiply_convert_fusion.6), channel_id=1, replica_groups=mesh['seq'=8,'head'=4] {'head'}, dimensions={0}, use_global_device_ids=true | all-gather | bytes 245760 | tf_op jit(solution)/shard_map/all_gather | solution.py:169
  324.2 11.6 %all-gather.2 = bf16[4,192,1,128]{3,1,0,2:T(8,128)(2,1)S(1)} all-gather(bf16[4,24,1,128]{3,1,0,2:T(8,128)(2,1)S(1)} %copy.61), channel_id=4, replica_groups=mesh['seq'=8,'head'=4] {'seq'}, dimensions={1}, use_global_device_ids=true | all-gather | bytes 221184 | tf_op jit(solution)/shard_map/all_gather | solution.py:181
  335.8 8.1 %all-gather.1 = bf16[4,192,1,128]{3,1,0,2:T(8,128)(2,1)S(1)} all-gather(bf16[4,24,1,128]{3,1,0,2:T(8,128)(2,1)S(1)} %copy.60), channel_id=3, replica_groups=mesh['seq'=8,'head'=4] {'seq'}, dimensions={1}, use_global_device_ids=true | all-gather | bytes 221184 | tf_op jit(solution)/shard_map/all_gather | solution.py:180
  (82 shorter events, 11.3 us)
Async XLA Ops:
  7.2 0.8 copy-start.6
  7.2 1.1 copy-start
  7.2 163.3 %all-gather.8.cloned.1.call-start = ((), (), s32[]{:S(2)}) async-start(), calls=%async_computation | async-start | bytes 11141120 | tf_op jit(solution)/shard_map/all_gather | solution.py:96
  7.9 209.9 %all-gather.12.cloned.1.call-start = ((), (), s32[]{:S(2)}) async-start(), calls=%async_computation.2 | async-start | bytes 4718592 | tf_op jit(solution)/shard_map/all_gather | solution.py:23
  8.4 169.0 %copy-start.5 = (f32[4,2304]{1,0:T(4,128)S(1)}, f32[4,2304]{1,0:T(4,128)}, u32[]{:S(2)}) copy-start(f32[4,2304]{1,0:T(4,128)} %param.14) | copy-start | bytes 110596
  175.5 2.8 collective-permute-start
  179.0 1.4 copy-start.1
  179.4 1.2 copy-start.2
  179.4 13.9 %copy-start.7 = (f32[2048]{0:T(1024)S(1)}, f32[2048]{0:T(1024)}, u32[]{:S(2)}) copy-start(f32[2048]{0:T(1024)} %param.15) | copy-start | bytes 24580
  180.5 12.9 %copy-start.8 = (s32[1,192]{1,0:T(1,128)S(1)}, s32[1,192]{1,0:T(1,128)}, u32[]{:S(2)}) copy-start(s32[1,192]{1,0:T(1,128)} %param.12) | copy-start | bytes 2308
  180.5 119.7 %all-gather.10.cloned.1.call-start = ((), (), s32[]{:S(2)}) async-start(), calls=%async_computation.1 | async-start | bytes 5242880 | tf_op jit(solution)/shard_map/all_gather | solution.py:138
  303.2 3.8 %copy-start.3 = (bf16[128,1024]{1,0:T(8,128)(2,1)}, bf16[128,1024]{1,0:T(8,128)(2,1)S(1)}, u32[]{:S(2)}) copy-start(bf16[128,1024]{1,0:T(8,128)(2,1)S(1)} %fusion.5) | copy-start | bytes 786436
  303.2 3.5 copy-start.4
  303.5 3.4 collective-permute-start.2
  305.3 4.4 %collective-permute-start.1 = (bf16[24,1024]{1,0:T(8,128)(2,1)S(1)}, bf16[24,1024]{1,0:T(8,128)(2,1)S(1)}, u32[]{:S(2)}, u32[]{:S(2)}) collective-permute-start(bf16[24,1024]{1,0:T(8,128)(2,1)S(1)} %get-tuple-element.158), channel_id=1, source_target_pairs={{4,0},{8,4},{12,8},{16,12},{20,16},{24,20},{28,24},{5,1},{9,5},{13... | collective-permute-start | bytes 147464 | tf_op jit(solution)/shard_map/ppermute | solution.py:17
Sparse Core Ops, SparseCore 0:
  9.6 160.8 all-gather.7
  180.6 37.1 all-gather.11
  219.4 80.7 all-gather.9
where the time goes:
time: 353 us; the launch traced here: 352 us
  waiting for transfers between devices  256 us (73%)
  blocking collectives  45.4 us (13%)
  matrix products  16.5 us (5%)
  between operations  14.1 us (4%)
  other arithmetic  12.9 us (4%)
  starting transfers between devices  5.12 us (1%)
    all_gather x1, waiting for transfers between devices, local(): lax.all_gather(in_weight, 'head', axis=0, tiled=True)  162 us
    all_gather x1, waiting for transfers between devices, local(): lax.all_gather(out_weight, 'head', axis=0, tiled=True)  69.8 us
    all_gather x1, waiting for transfers between devices, entering(): lax.all_gather(part.astype(kind), axis)  19.4 us
    all_gather x1, blocking collectives, local(): lax.all_gather(group_normed, 'head', axis=0, tiled=True)  13.8 us
    all_gather x1, blocking collectives, entering(): lax.all_gather(part.astype(kind), axis)  11.9 us
    all_gather x1, blocking collectives, local(): value_piece = lax.all_gather(values, 'seq', axis=1, tiled=True)  11.6 us
    select_n x8, other arithmetic, lap(): return jax.tree.map(lambda a, b: jnp.where(reached, a, b), new, before)  10.5 us
    all_gather x1, blocking collectives, local(): key_fragment = lax.all_gather(key_rows, 'seq', axis=1, tiled=True)  8.11 us
  transfers between devices with their start and end apart: 6, of which 5 were waited for; matrix products, arithmetic and copies ran while one was open for 5% of the time, Pallas kernels for 0%

commit v1 on v0

--- a/solution.py
+++ b/solution.py
@@ -36,9 +36,16 @@
     return lax.fori_loop(0, length, lap, start)
 
 
+def running_sum(values):
+    length = values.shape[0]
+    row = lax.broadcasted_iota(jnp.int32, (length, length), 0)
+    column = lax.broadcasted_iota(jnp.int32, (length, length), 1)
+    return jnp.dot((column <= row).astype(jnp.float32), values, precision=highest)
+
+
 def state_block(hidden_state, block_items):
     head_inputs, write_vectors, read_vectors, decays = block_items
-    cumulative = jnp.cumsum(decays, axis=0)
+    cumulative = running_sum(decays)
     length = decays.shape[0]
     later_index = lax.broadcasted_iota(jnp.int32, (length, length), 0)
     earlier_index = lax.broadcasted_iota(jnp.int32, (length, length), 1)
@@ -117,7 +124,7 @@
     )
     local_state, outputs = lax.scan(state_block, start_state, block_items)
     outputs = outputs.reshape(row_count, head_count, head_dim)
-    cumulative = jnp.cumsum(decays, axis=0)
+    cumulative = running_sum(decays)
     identity = (jnp.zeros((head_count,), jnp.float32), jnp.zeros_like(local_state))
     carried = entering((cumulative[-1], local_state), "seq", combine_states, identity)
     outputs = outputs + jnp.exp(cumulative)[:, :, None] * jnp.einsum(

time: 353 us -> 353 us (level)
  waiting for transfers between devices: 256 us -> 249 us
  other arithmetic: 12.9 us -> 19.5 us
    exp x8, other arithmetic: 0.07 us -> 5.54 us  [combine_states(): jnp.exp(later[0])[:, None, None] * earlier[1] + later[1]]
    all_gather x1, waiting for transfers between devices: 69.8 us -> 64.4 us  [local(): lax.all_gather(out_weight, 'head', axis=0, tiled=True)]
  transfers between devices with their start and end apart: 6 -> 6, of which waited for: 5 -> 5; matrix products, arithmetic and copies ran while one was open for 5% -> 7% of each run, Pallas kernels for 0% -> 0%
where the time goes in v1:
time: 353 us; the launch traced here: 352 us
  waiting for transfers between devices  249 us (71%)
  blocking collectives  45.4 us (13%)
  other arithmetic  19.5 us (6%)
  matrix products  16.6 us (5%)
  between operations  14.1 us (4%)
  starting transfers between devices  5.12 us (1%)
    all_gather x1, waiting for transfers between devices, local(): lax.all_gather(in_weight, 'head', axis=0, tiled=True)  162 us
    all_gather x1, waiting for transfers between devices, local(): lax.all_gather(out_weight, 'head', axis=0, tiled=True)  64.4 us
    all_gather x1, waiting for transfers between devices, entering(): lax.all_gather(part.astype(kind), axis)  17.6 us
    all_gather x1, blocking collectives, local(): lax.all_gather(group_normed, 'head', axis=0, tiled=True)  13.8 us
    all_gather x1, blocking collectives, entering(): lax.all_gather(part.astype(kind), axis)  11.9 us
    all_gather x1, blocking collectives, local(): value_piece = lax.all_gather(values, 'seq', axis=1, tiled=True)  11.6 us
    select_n x8, other arithmetic, lap(): return jax.tree.map(lambda a, b: jnp.where(reached, a, b), new, before)  10.5 us
    all_gather x1, blocking collectives, local(): key_fragment = lax.all_gather(key_rows, 'seq', axis=1, tiled=True)  8.11 us
  transfers between devices with their start and end apart: 6, of which 5 were waited for; matrix products, arithmetic and copies ran while one was open for 7% of the time, Pallas kernels for 0%

profile of v1, /device:TPU:0, one launch (start us, length us, event | category | flops | bytes accessed | tf_op | source)
XLA Modules:
  0.0 351.8 jit_solution(10230298177922761636)
XLA Ops:
  8.6 161.9 %all-gather.8.cloned.1.call-done = bf16[1024,4352]{1,0:T(8,128)(2,1)} async-done(((bf16[256,4352]{1,0:T(8,128)(2,1)}), bf16[1024,4352]{1,0:T(8,128)(2,1)}) %all-gather.8.cloned.1.call-update) | async-done | bytes 8912912 | tf_op jit(solution)/shard_map/all_gather | solution.py:103
  170.5 4.9 %convolution_convert_fusion = bf16[128,4352]{1,0:T(8,128)(2,1)S(1)} fusion(bf16[1024,4352]{1,0:T(8,128)(2,1)} %all-gather.8.cloned.1.call-done, bf16[1,128,1024]{2,1,0:T(8,128)(2,1)S(1)} %copy-done.1, f32[128]{0:T(128)S(1)} %add_rsqrt_fusion.2), kind=kOutput, calls=%fused_computation.3 | convolution fusion | flops 1141800960 | bytes 10289664 | tf_op jit(solution)/shard_map/dot_general | solution.py:101
  175.5 2.0 collective-permute-start
  181.5 11.9 %all-gather.3 = bf16[8,1,32]{2,1,0:T(2,128)(2,1)S(1)} all-gather(bf16[1,1,32]{2,1,0:T(2,128)(2,1)S(1)} %bitcast.78), channel_id=1, replica_groups=mesh['seq'=8,'head'=4] {'seq'}, dimensions={0}, use_global_device_ids=true | all-gather | bytes 576 | tf_op jit(solution)/shard_map/all_gather | solution.py:23
  196.9 2.1 convolution_bitcast_fusion
  198.9 1.3 fusion.2
  200.3 17.6 %all-gather.12.cloned.1.call-done = bf16[256,64,128]{2,1,0:T(8,128)(2,1)} async-done(((bf16[32,64,128]{2,1,0:T(8,128)(2,1)}), bf16[256,64,128]{2,1,0:T(8,128)(2,1)}) %all-gather.12.cloned.1.call-update) | async-done | bytes 4194320 | tf_op jit(solution)/shard_map/all_gather | solution.py:23
  217.9 16.2 %while.9 = (s32[]{:T(128)}, f32[32,64,128]{2,1,0:T(8,128)S(1)}, s32[]{:T(128)}, bf16[8,32]{1,0:T(8,128)(2,1)}, bf16[8,32,64,128]{3,2,1,0:T(8,128)(2,1)}, /*index=5*/s32[]{:T(128)}, s32[]{:T(128)}) while((s32[]{:T(128)}, f32[32,64,128]{2,1,0:T(8,128)S(1)}, s32[]{:T(128)}, bf16[8,32]{1,0:T(8,128)(2,1)}, ...), condition=%wide.region_2.3_spmd.clone, body=%wide.region_1.2_spmd.clone.sunk | while | flops 1310756 | bytes 2621873 | solution.py:36
  218.6 1.3 fusion.63
  220.6 1.3 fusion.63
  222.6 1.3 fusion.63
  224.6 1.3 fusion.63
  226.6 1.4 fusion.63
  228.7 1.4 fusion.63
  230.7 1.3 fusion.63
  232.7 1.3 fusion.63
  234.1 1.5 multiply_reduce_fusion
  235.9 64.4 %all-gather.10.cloned.1.call-done = bf16[2048,1024]{1,0:T(8,128)(2,1)} async-done(((bf16[512,1024]{1,0:T(8,128)(2,1)}), bf16[2048,1024]{1,0:T(8,128)(2,1)}) %all-gather.10.cloned.1.call-update) | async-done | bytes 4194320 | tf_op jit(solution)/shard_map/all_gather | solution.py:145
  300.3 2.9 fusion.5
  303.5 1.8 collective-permute-start.2
  307.0 2.7 collective-permute-done.1
  309.9 13.8 %all_gather.30 = bf16[96,1024]{1,0:T(8,128)(2,1)S(1)} all-gather(bf16[24,1024]{1,0:T(8,128)(2,1)S(1)} %multiply_convert_fusion.6), channel_id=1, replica_groups=mesh['seq'=8,'head'=4] {'head'}, dimensions={0}, use_global_device_ids=true | all-gather | bytes 245760 | tf_op jit(solution)/shard_map/all_gather | solution.py:176
  324.2 11.6 %all-gather.2 = bf16[4,192,1,128]{3,1,0,2:T(8,128)(2,1)S(1)} all-gather(bf16[4,24,1,128]{3,1,0,2:T(8,128)(2,1)S(1)} %copy.41), channel_id=4, replica_groups=mesh['seq'=8,'head'=4] {'seq'}, dimensions={1}, use_global_device_ids=true | all-gather | bytes 221184 | tf_op jit(solution)/shard_map/all_gather | solution.py:188
  335.9 8.1 %all-gather.1 = bf16[4,192,1,128]{3,1,0,2:T(8,128)(2,1)S(1)} all-gather(bf16[4,24,1,128]{3,1,0,2:T(8,128)(2,1)S(1)} %copy.40), channel_id=3, replica_groups=mesh['seq'=8,'head'=4] {'seq'}, dimensions={1}, use_global_device_ids=true | all-gather | bytes 221184 | tf_op jit(solution)/shard_map/all_gather | solution.py:187
  (82 shorter events, 18.7 us)
Async XLA Ops:
  7.2 0.8 copy-start
  7.2 1.2 copy-start.1
  7.2 163.3 %all-gather.8.cloned.1.call-start = ((), (), s32[]{:S(2)}) async-start(), calls=%async_computation | async-start | bytes 11141120 | tf_op jit(solution)/shard_map/all_gather | solution.py:103
  7.9 209.9 %all-gather.12.cloned.1.call-start = ((), (), s32[]{:S(2)}) async-start(), calls=%async_computation.2 | async-start | bytes 4718592 | tf_op jit(solution)/shard_map/all_gather | solution.py:23
  8.6 168.8 %copy-start.6 = (f32[4,2304]{1,0:T(4,128)S(1)}, f32[4,2304]{1,0:T(4,128)}, u32[]{:S(2)}) copy-start(f32[4,2304]{1,0:T(4,128)} %param.14) | copy-start | bytes 110596
  175.5 2.8 collective-permute-start
  179.0 1.4 copy-start.2
  179.4 1.9 copy-start.3
  179.4 14.6 %copy-start.7 = (f32[2048]{0:T(1024)S(1)}, f32[2048]{0:T(1024)}, u32[]{:S(2)}) copy-start(f32[2048]{0:T(1024)} %param.15) | copy-start | bytes 24580
  179.4 15.2 %copy-start.8 = (s32[1,192]{1,0:T(1,128)S(1)}, s32[1,192]{1,0:T(1,128)}, u32[]{:S(2)}) copy-start(s32[1,192]{1,0:T(1,128)} %param.12) | copy-start | bytes 2308
  180.5 119.7 %all-gather.10.cloned.1.call-start = ((), (), s32[]{:S(2)}) async-start(), calls=%async_computation.1 | async-start | bytes 5242880 | tf_op jit(solution)/shard_map/all_gather | solution.py:145
  300.2 2.9 copy-start.9
  300.2 6.4 %copy-start.10 = (s32[24]{0:T(128)S(1)}, s32[24]{0:T(128)}, u32[]{:S(2)}) copy-start(s32[24]{0:T(128)} %iota_add_fusion.1) | copy-start | bytes 292
  303.2 3.8 %copy-start.4 = (bf16[128,1024]{1,0:T(8,128)(2,1)}, bf16[128,1024]{1,0:T(8,128)(2,1)S(1)}, u32[]{:S(2)}) copy-start(bf16[128,1024]{1,0:T(8,128)(2,1)S(1)} %fusion.5) | copy-start | bytes 786436
  303.2 3.5 copy-start.5
  303.5 3.4 collective-permute-start.2
  305.3 4.4 %collective-permute-start.1 = (bf16[24,1024]{1,0:T(8,128)(2,1)S(1)}, bf16[24,1024]{1,0:T(8,128)(2,1)S(1)}, u32[]{:S(2)}, u32[]{:S(2)}) collective-permute-start(bf16[24,1024]{1,0:T(8,128)(2,1)S(1)} %get-tuple-element.158), channel_id=1, source_target_pairs={{4,0},{8,4},{12,8},{16,12},{20,16},{24,20},{28,24},{5,1},{9,5},{13... | collective-permute-start | bytes 147464 | tf_op jit(solution)/shard_map/ppermute | solution.py:17
Sparse Core Ops, SparseCore 0:
  9.6 160.8 all-gather.7
  180.6 37.1 all-gather.11
  219.4 80.7 all-gather.9

commit v2 on v0

v2 whole, which is shorter than its diff:
```python
import math

import jax
import jax.numpy as jnp
from jax import lax
from jax.sharding import PartitionSpec as P

BLOCK = 128


highest = lax.Precision.HIGHEST


def passed_along(value, axis, steps):
    count = lax.axis_size(axis)
    first, last = (max(0, -steps), min(count, count - steps))
    return lax.ppermute(value, axis, [(source, source + steps) for source in range(first, last)])


def convolve(padded, conv_weight, length):
    summed = jnp.zeros((length, padded.shape[1]), jnp.float32)
    for offset in range(conv_weight.shape[0]):
        summed = summed + conv_weight[offset] * padded[offset : offset + length].astype(jnp.float32)
    return jax.nn.silu(summed).astype(jnp.bfloat16)


def pieces(values):
    parts, rest = [], values
    for _ in range(3):
        part = lax.reduce_precision(rest, 8, 7)
        parts.append(part.astype(jnp.bfloat16))
        rest = rest - part
    return parts


def head_columns(array, first, own_heads, head_dim, axis):
    return jnp.concatenate(
        [
            lax.dynamic_slice_in_dim(array, first + head * head_dim, head_dim, axis)
            for head in own_heads
        ],
        axis=axis,
    )


def mix(head_inputs, write_vectors, read_vectors, decays):
    blocks, length, heads, head_dim = head_inputs.shape
    later = lax.broadcasted_iota(jnp.int32, (length, length), 0)
    earlier = lax.broadcasted_iota(jnp.int32, (length, length), 1)
    causal = earlier <= later
    cumulative = jnp.einsum(
        "ts,bsh->bht", causal.astype(jnp.float32), decays, precision=highest
    )
    spread = cumulative[:, :, :, None] - cumulative[:, :, None, :]
    factor = jnp.where(causal, jnp.exp(jnp.where(causal, spread, 0.0)), 0.0)
    gram_matrix = jnp.einsum(
        "btn,bsn->bts", read_vectors, write_vectors, preferred_element_type=jnp.float32
    )
    mixed = (factor * gram_matrix[:, None]).astype(jnp.bfloat16)
    output = jnp.einsum("bhts,bshp->bhtp", mixed, head_inputs, preferred_element_type=jnp.float32)
    final_log = cumulative[:, :, -1]
    tail_decay = jnp.exp(final_log[:, :, None] - cumulative)
    weighted = (
        head_inputs.astype(jnp.float32) * tail_decay.transpose(0, 2, 1)[..., None]
    ).astype(jnp.bfloat16)
    fresh = jnp.einsum(
        "bshp,bsn->bhpn", weighted, write_vectors, preferred_element_type=jnp.float32
    )
    state = jnp.zeros_like(fresh[0])
    before = []
    for block in range(blocks):
        before.append(state.astype(jnp.bfloat16))
        state = jnp.exp(final_log[block])[:, None, None] * state + fresh[block]
    carried = jnp.einsum(
        "btn,bhpn->bhtp", read_vectors, jnp.stack(before), preferred_element_type=jnp.float32
    )
    return output + jnp.exp(cumulative)[..., None] * carried


def encode(states, decays, in_weight, conv_weight, norm_gain, out_weight):
    row_count, model_width = states.shape
    head_count = decays.shape[1]
    inner_width = norm_gain.shape[0]
    head_dim = inner_width // head_count
    state_width = (in_weight.shape[1] - 2 * inner_width) // 2
    seq_count, place = lax.axis_size("seq"), lax.axis_index("seq")
    depth_count, depth = lax.axis_size("head"), lax.axis_index("head")
    heads = head_count // seq_count
    shard_heads = head_count // depth_count
    spread_out = shard_heads % seq_count == 0
    if spread_out:
        own_heads = [place + seq_count * k for k in range(heads)]
    else:
        own_heads = [place * heads + k for k in range(heads)]
    weight = jnp.concatenate(
        [
            head_columns(in_weight, 0, own_heads, head_dim, 1),
            head_columns(in_weight, inner_width, own_heads, head_dim, 1),
            in_weight[:, 2 * inner_width :],
        ],
        axis=1,
    )
    weight = lax.all_gather(weight, "head", axis=0, tiled=True)
    if spread_out:
        here = [place + seq_count * k for k in range(shard_heads // seq_count)]
        back = lax.all_gather(
            head_columns(out_weight, 0, here, head_dim, 0), "head", axis=0, tiled=True
        )
    else:
        rows = heads * head_dim
        owner = (place * rows) // out_weight.shape[0]
        slab = lax.dynamic_slice_in_dim(out_weight, place * rows - owner * out_weight.shape[0], rows)
        back = lax.psum(jnp.where(owner == depth, slab, jnp.zeros_like(slab)), "head")
    float_states = states.astype(jnp.float32)
    normed = (
        float_states
        * lax.rsqrt(jnp.mean(float_states * float_states, axis=-1, keepdims=True) + 1e-05)
    ).astype(jnp.bfloat16)
    gathered = lax.all_gather(
        jnp.concatenate([normed, *pieces(decays)], axis=1), "seq", axis=0, tiled=True
    )
    length = gathered.shape[0]
    projected = jnp.dot(
        gathered[:, :model_width], weight, preferred_element_type=jnp.float32
    ).astype(jnp.bfloat16)
    high, middle, low = (
        head_columns(
            gathered[:, model_width + k * head_count : model_width + (k + 1) * head_count],
            0, own_heads, 1, 1,
        ).astype(jnp.float32)
        for k in range(3)
    )
    own_decays = high + (middle + low)
    width = heads * head_dim
    mixer_in = projected[:, width:]
    taps = jnp.concatenate(
        [
            head_columns(conv_weight, 0, own_heads, head_dim, 1),
            conv_weight[:, inner_width:],
        ],
        axis=1,
    )
    padded = jnp.concatenate(
        [jnp.zeros((conv_weight.shape[0] - 1, mixer_in.shape[1]), jnp.bfloat16), mixer_in], axis=0
    )
    convolved = convolve(padded, taps, length)
    blocks = length // BLOCK
    mixed = mix(
        convolved[:, :width].reshape(blocks, BLOCK, heads, head_dim),
        convolved[:, width : width + state_width].reshape(blocks, BLOCK, state_width),
        convolved[:, width + state_width :].reshape(blocks, BLOCK, state_width),
        own_decays.reshape(blocks, BLOCK, heads),
    )
    gate = projected[:, :width].reshape(blocks, BLOCK, heads, head_dim).transpose(0, 2, 1, 3)
    gated = mixed * jax.nn.silu(gate.astype(jnp.float32))
    gain = head_columns(norm_gain, 0, own_heads, head_dim, 0).reshape(heads, 1, head_dim)
    scaled = (
        gated * lax.rsqrt(jnp.mean(gated * gated, axis=-1, keepdims=True) + 1e-05) * gain
    ).astype(jnp.bfloat16)
    flat = scaled.transpose(0, 2, 1, 3).reshape(length, width)
    share = jnp.dot(flat, back, preferred_element_type=jnp.float32).astype(jnp.bfloat16)
    branch = lax.psum_scatter(share, "seq", scatter_dimension=0, tiled=True)
    return (float_states + branch.astype(jnp.float32)).astype(jnp.bfloat16)


def local(
    byte_states, log_decay, group_starts, in_weight, conv_weight, norm_gain, out_weight, qkv_weight
):
    states = byte_states[0]
    starts = group_starts[0]
    row_count, model_width = states.shape
    encoded = encode(states, log_decay[0], in_weight, conv_weight, norm_gain, out_weight)
    seq_count = lax.axis_size("seq")
    seq_index = lax.axis_index("seq")
    groups = starts.shape[0]
    per_device = groups // seq_count
    positions = seq_index * row_count + jnp.arange(row_count, dtype=jnp.int32)
    group_id = jnp.sum((starts[None, :] <= positions[:, None]).astype(jnp.int32), axis=1) - 1
    contract_rows = (((0,), (0,)), ((), ()))
    local_id = group_id - (seq_index - 1) * per_device
    onehot = (local_id[:, None] == jnp.arange(3 * per_device, dtype=jnp.int32)[None, :]).astype(
        jnp.bfloat16
    )
    partial_value = lax.dot_general(
        onehot, encoded, contract_rows, preferred_element_type=jnp.float32
    )
    from_above = passed_along(partial_value[:per_device].astype(jnp.bfloat16), "seq", -1).astype(
        jnp.float32
    )
    from_below = passed_along(
        partial_value[2 * per_device :].astype(jnp.bfloat16), "seq", 1
    ).astype(jnp.float32)
    pooled = partial_value[per_device : 2 * per_device] + from_above + from_below
    group_normed = (
        pooled * lax.rsqrt(jnp.mean(pooled * pooled, axis=-1, keepdims=True) + 1e-05)
    ).astype(jnp.bfloat16)
    key_width = qkv_weight.shape[3]
    projection = qkv_weight.reshape(model_width, 3 * key_width)
    triple = jnp.dot(
        lax.all_gather(group_normed, "head", axis=0, tiled=True),
        projection,
        preferred_element_type=jnp.float32,
    ).astype(jnp.bfloat16)
    batch_rows = lax.axis_size("head")
    triple = triple.reshape(batch_rows, per_device, 3, key_width)
    query_rows = triple[:, :, 0]
    key_rows = triple[:, :, 1]
    values = triple[:, :, 2]
    query_pos = seq_index * per_device + jnp.arange(per_device, dtype=jnp.int32)
    row_max = jnp.full((batch_rows, per_device), -1e30, jnp.float32)
    key_fragment = lax.all_gather(key_rows, "seq", axis=1, tiled=True)
    value_piece = lax.all_gather(values, "seq", axis=1, tiled=True)
    key_count = key_fragment.shape[1]
    scores = jnp.einsum(
        "tfv,tuv->tfu", query_rows, key_fragment, preferred_element_type=jnp.float32
    ) / math.sqrt(key_width)
    key_pos = jnp.arange(key_count, dtype=jnp.int32)
    allowed = key_pos[None, None, :] <= query_pos[None, :, None]
    new_max = jnp.maximum(row_max, jnp.max(jnp.where(allowed, scores, -1e30), axis=-1))
    exp_scores = jnp.where(
        allowed, jnp.exp(jnp.where(allowed, scores - new_max[:, :, None], 0.0)), 0.0
    )
    row_total = jnp.sum(exp_scores, axis=-1)
    summed = jnp.einsum(
        "vhf,vfy->vhy",
        exp_scores.astype(jnp.bfloat16),
        value_piece,
        preferred_element_type=jnp.float32,
    )
    row_max, row_total, summed = (new_max, row_total, summed)
    attended = (
        (summed / row_total[:, :, None])
        .astype(jnp.bfloat16)
        .reshape(batch_rows, per_device, 1, key_width)
    )
    return (encoded[None], attended)


def solution(mesh):
    placed = (
        P("head", "seq", None),
        P("head", "seq", None),
        P("head", None),
        P("head", None),
        P(),
        P(),
        P("head", None),
        P(None, None, "head", None),
    )
    return jax.shard_map(
        local,
        mesh=mesh,
        in_specs=placed,
        out_specs=(P("head", "seq", None), P(None, "seq", "head", None)),
        check_vma=False,
    )
```

time: 353 us -> 204 us (0.58)
  waiting for transfers between devices: 256 us -> 88.9 us
  local copies, waits for them, and re-layouts: 1.65 us -> 17.6 us
  blocking collectives: 45.4 us -> 58.4 us
  other arithmetic: 12.9 us -> 7.83 us
  matrix products: 16.5 us -> 11.8 us
    all_gather x3 -> x2, waiting for transfers between devices: 251 us -> 48.3 us  [the longest x1 31.6 us: encode(): lax.all_gather(jnp.concatenate([normed, *pieces(decays)], axis=1), 'seq',...]
    reduce_scatter x0 -> x1, waiting for transfers between devices: none -> 40.5 us  [encode(): branch = lax.psum_scatter(share, 'seq', scatter_dimension=0, tiled=True)]
    all_gather x1, blocking collectives: 11.9 us -> 24.2 us  [encode(): lax.all_gather(head_columns(out_weight, 0, here, head_dim, 0), 'head', ax...]
    select_n x8 -> x0, other arithmetic: 10.5 us -> none  [lap(): return jax.tree.map(lambda a, b: jnp.where(reached, a, b), new, before)]
    dot_general x7, matrix products: 14.7 us -> 9.07 us  [the longest x1 3.82 us: encode(): jnp.dot(gathered[:, :model_width], weight, preferred_element_type=jnp.flo...]
    convert_element_type x0 -> x6, local copies, waits for them, and re-layouts: none -> 4.39 us  [the longest x2 3.69 us: encode(): gated = mixed * jax.nn.silu(gate.astype(jnp.float32))]
    dynamic_slice x0 -> x6, local copies, waits for them, and re-layouts: none -> 4.33 us  [head_columns(): lax.dynamic_slice_in_dim(array, first + head * head_dim, head_dim, axis)]
    all_gather x1, blocking collectives: 8.11 us -> 12.2 us  [local(): key_fragment = lax.all_gather(key_rows, 'seq', axis=1, tiled=True)]
  transfers between devices with their start and end apart: 6 -> 5, of which waited for: 5 -> 3; matrix products, arithmetic and copies ran while one was open for 5% -> 3% of each run, Pallas kernels for 0% -> 0%
where the time goes in v2:
time: 204 us; the launch traced here: 203 us
  waiting for transfers between devices  88.9 us (44%)
  blocking collectives  58.4 us (29%)
  local copies, waits for them, and re-layouts  17.6 us (9%)
  between operations  14.2 us (7%)
  matrix products  11.8 us (6%)
  other arithmetic  7.83 us (4%)
  starting transfers between devices  4.45 us (2%)
    reduce_scatter x1, waiting for transfers between devices, encode(): branch = lax.psum_scatter(share, 'seq', scatter_dimension=0, tiled=True)  40.5 us
    all_gather x1, waiting for transfers between devices, encode(): lax.all_gather(jnp.concatenate([normed, *pieces(decays)], axis=1), 'seq',...  31.6 us
    all_gather x1, blocking collectives, encode(): lax.all_gather(head_columns(out_weight, 0, here, head_dim, 0), 'head', ax...  24.2 us
    all_gather x1, waiting for transfers between devices, encode(): weight = lax.all_gather(weight, 'head', axis=0, tiled=True)  16.6 us
    all_gather x1, blocking collectives, local(): lax.all_gather(group_normed, 'head', axis=0, tiled=True)  13.9 us
    all_gather x1, blocking collectives, local(): key_fragment = lax.all_gather(key_rows, 'seq', axis=1, tiled=True)  12.2 us
    all_gather x1, blocking collectives, local(): value_piece = lax.all_gather(values, 'seq', axis=1, tiled=True)  8.11 us
    dynamic_slice x6, local copies, waits for them, and re-layouts, head_columns(): lax.dynamic_slice_in_dim(array, first + head * head_dim, head_dim, axis)  4.33 us
  transfers between devices with their start and end apart: 5, of which 3 were waited for; matrix products, arithmetic and copies ran while one was open for 3% of the time, Pallas kernels for 0%

profile of v2, /device:TPU:0, one launch (start us, length us, event | category | flops | bytes accessed | tf_op | source)
XLA Modules:
  0.0 203.1 jit_solution(3820521602870420839)
XLA Ops:
  7.3 1.0 slice.139
  8.3 1.3 constant_dynamic-slice_fusion.1
  14.1 24.2 %all_gather.20 = bf16[256,1024]{1,0:T(8,128)(2,1)} all-gather(bf16[64,1024]{1,0:T(8,128)(2,1)S(1)} %constant_dynamic-slice_fusion), channel_id=1, replica_groups=mesh['seq'=8,'head'=4] {'head'}, dimensions={0}, use_global_device_ids=true | all-gather | bytes 655360 | tf_op jit(solution)/shard_map/all_gather | solution.py:106
  38.2 16.6 %all-gather.7.cloned.1.call-done = bf16[1024,768]{1,0:T(8,128)(2,1)} async-done(((bf16[256,768]{1,0:T(8,128)(2,1)}), bf16[1024,768]{1,0:T(8,128)(2,1)}) %all-gather.7.cloned.1.call-update) | async-done | bytes 1572880 | tf_op jit(solution)/shard_map/all_gather | solution.py:103
  54.9 31.6 %all-gather.5.cloned.1.call-done = bf16[1024,1120]{1,0:T(8,128)(2,1)} async-done(((bf16[128,1120]{1,0:T(8,128)(2,1)}), bf16[1024,1120]{1,0:T(8,128)(2,1)}) %all-gather.5.cloned.1.call-update) | async-done | bytes 2293776 | tf_op jit(solution)/shard_map/all_gather | solution.py:119
  86.5 3.8 %fusion.2 = bf16[1024,768]{1,0:T(8,128)(2,1)S(1)} fusion(bf16[1024,768]{1,0:T(8,128)(2,1)} %all-gather.7.cloned.1.call-done, bf16[1024,1120]{1,0:T(8,128)(2,1)} %all-gather.5.cloned.1.call-done), kind=kOutput, calls=%fused_computation.5 | convolution fusion | flops 1611399168 | bytes 5242880 | tf_op jit(solution)/shard_map/dot_general | solution.py:123
  90.4 1.3 multiply_convert_fusion.1
  92.7 1.5 fusion.90
  94.9 1.3 dynamic-slice_reduce_fusion.3
  96.8 1.1 slice_convert_fusion
  99.1 2.1 %reshape.187 = f32[8,128,4,64]{3,2,1,0:T(4,128)S(1)} reshape(f32[1024,256]{1,0:T(8,128)} %slice_convert_fusion) | data formatting | bytes 2097152 | tf_op jit(solution)/shard_map/convert_element_type | solution.py:155
  101.2 1.6 copy.72
  102.8 1.2 multiply_convert_fusion.3
  104.0 1.3 fusion.29
  107.1 1.2 fusion.22
  109.4 2.1 %convolution_convert_fusion = bf16[1024,1024]{1,0:T(8,128)(2,1)} fusion(bf16[256,1024]{1,0:T(8,128)(2,1)S(1)} %copy-done.6, bf16[32,8,8,128]{3,2,1,0:T(8,128)(2,1)S(1)} %bitcast.139), kind=kOutput, calls=%fused_computation.4 | convolution fusion | flops 537919488 | bytes 3145728 | tf_op jit(solution)/shard_map/dot_general | solution.py:161
  112.3 40.5 %reduce-scatter.2.cloned.1.call-done = bf16[128,1024]{1,0:T(8,128)(2,1)} async-done(((bf16[1024,1024]{1,0:T(8,128)(2,1)}), bf16[128,1024]{1,0:T(8,128)(2,1)}) %reduce-scatter.2.cloned.1.call-update) | async-done | bytes 262160 | tf_op jit(solution)/shard_map/reduce_scatter | solution.py:162
  152.9 1.3 fusion.96
  154.2 1.3 collective-permute-start
  155.5 3.0 %collective-permute-start.1 = (bf16[24,1024]{1,0:T(8,128)(2,1)S(1)}, bf16[24,1024]{1,0:T(8,128)(2,1)S(1)}, u32[]{:S(2)}, u32[]{:S(2)}) collective-permute-start(bf16[24,1024]{1,0:T(8,128)(2,1)S(1)} %get-tuple-element.49), channel_id=1, source_target_pairs={{0,4},{4,8},{8,12},{12,16},{16,20},{20,24},{24,28},{1,5},{5,9},{9,... | collective-permute-start | bytes 147464 | tf_op jit(solution)/shard_map/ppermute | solution.py:17
  158.5 1.7 fusion.38
  160.5 13.9 %all_gather.21 = bf16[96,1024]{1,0:T(8,128)(2,1)S(1)} all-gather(bf16[24,1024]{1,0:T(8,128)(2,1)S(1)} %multiply_convert_fusion.4), channel_id=1, replica_groups=mesh['seq'=8,'head'=4] {'head'}, dimensions={0}, use_global_device_ids=true | all-gather | bytes 245760 | tf_op jit(solution)/shard_map/all_gather | solution.py:200
  174.9 12.2 %all-gather = bf16[4,192,1,128]{3,1,0,2:T(8,128)(2,1)S(1)} all-gather(bf16[4,24,1,128]{3,1,0,2:T(8,128)(2,1)S(1)} %copy.86), channel_id=2, replica_groups=mesh['seq'=8,'head'=4] {'seq'}, dimensions={1}, use_global_device_ids=true | all-gather | bytes 221184 | tf_op jit(solution)/shard_map/all_gather | solution.py:211
  187.5 8.1 %all-gather.1 = bf16[4,192,1,128]{3,1,0,2:T(8,128)(2,1)S(1)} all-gather(bf16[4,24,1,128]{3,1,0,2:T(8,128)(2,1)S(1)} %copy.87), channel_id=3, replica_groups=mesh['seq'=8,'head'=4] {'seq'}, dimensions={1}, use_global_device_ids=true | all-gather | bytes 221184 | tf_op jit(solution)/shard_map/all_gather | solution.py:212
  (99 shorter events, 13.7 us)
Async XLA Ops:
  7.2 6.9 %copy-start = (bf16[512,1024]{1,0:T(8,128)(2,1)S(1)}, bf16[512,1024]{1,0:T(8,128)(2,1)}, u32[]{:S(2)}) copy-start(bf16[512,1024]{1,0:T(8,128)(2,1)} %param.14) | copy-start | bytes 3145732
  7.2 3.5 %copy-start.11 = (f32[1,128,32]{1,2,0:T(8,128)S(1)}, f32[1,128,32]{1,2,0:T(8,128)}, u32[]{:S(2)}) copy-start(f32[1,128,32]{1,2,0:T(8,128)} %param.9) | copy-start | bytes 49156
  7.2 3.8 %copy-start.2 = (bf16[1,128,1024]{2,1,0:T(8,128)(2,1)S(1)}, bf16[1,128,1024]{2,1,0:T(8,128)(2,1)}, u32[]{:S(2)}) copy-start(bf16[1,128,1024]{2,1,0:T(8,128)(2,1)} %param.8) | copy-start | bytes 786436
  7.2 47.7 %all-gather.7.cloned.1.call-start = ((), (), s32[]{:S(2)}) async-start(), calls=%async_computation.2 | async-start | bytes 1966080 | tf_op jit(solution)/shard_map/all_gather | solution.py:103
  8.3 5.0 %copy-start.10 = (f32[4,2304]{1,0:T(4,128)S(1)}, f32[4,2304]{1,0:T(4,128)}, u32[]{:S(2)}) copy-start(f32[4,2304]{1,0:T(4,128)} %param.12) | copy-start | bytes 110596
  8.3 5.0 %slice-start.1 = ((f32[4,2304]{1,0:T(4,128)}), f32[4,256]{1,0:T(4,128)S(1)}, s32[]{:S(2)}) async-start(f32[4,2304]{1,0:T(4,128)} %param.12), calls=%async_computation.5 | async-start | bytes 8192 | tf_op jit(solution)/shard_map/slice | solution.py:139
  10.6 75.9 %all-gather.5.cloned.1.call-start = ((), (), s32[]{:S(2)}) async-start(), calls=%async_computation.1 | async-start | bytes 2654208 | tf_op jit(solution)/shard_map/all_gather | solution.py:119
  12.2 140.7 %reduce-scatter.2.cloned.1.call-start = ((), (), s32[]{:S(2)}) async-start(), calls=%async_computation.3 | async-start | bytes 2359296 | tf_op jit(solution)/shard_map/reduce_scatter | solution.py:162
  91.8 3.2 %copy-start.3 = (bf16[1024,512]{1,0:T(8,128)(2,1)}, bf16[1024,512]{1,0:T(8,128)(2,1)S(1)}, u32[]{:S(2)}) copy-start(bf16[1024,512]{1,0:T(8,128)(2,1)S(1)} %multiply_convert_fusion.1) | copy-start | bytes 3145732
  94.9 3.1 %slice-start = ((bf16[1024,512]{1,0:T(8,128)(2,1)}), bf16[1024,256]{1,0:T(8,128)(2,1)S(1)}, s32[]{:S(2)}) async-start(bf16[1024,512]{1,0:T(8,128)(2,1)} %copy-done.3), calls=%async_computation.4 | async-start | bytes 1048576 | tf_op jit(solution)/shard_map/slice | solution.py:149
  102.8 2.5 %copy-start.9 = (bf16[8,4,64,128]{3,2,1,0:T(8,128)(2,1)S(1)}, bf16[8,4,64,128]{3,2,1,0:T(8,128)(2,1)}, u32[]{:S(2)}) copy-start(bf16[8,4,64,128]{3,2,1,0:T(8,128)(2,1)} %broadcast_dynamic-update-slice_fusion) | copy-start | bytes 1572868
  104.0 2.1 %copy-start.4 = (bf16[1024,128]{1,0:T(8,128)(2,1)S(1)}, bf16[1024,128]{1,0:T(8,128)(2,1)}, u32[]{:S(2)}) copy-start(bf16[1024,128]{1,0:T(8,128)(2,1)} %get-tuple-element.46) | copy-start | bytes 786436
  105.5 1.0 copy-start.5
  105.8 1.2 copy-start.1
  105.8 1.4 copy-start.7
  108.3 1.0 copy-start.6
  109.4 2.1 %copy-start.8 = (bf16[1024,3,1,128]{3,0,2,1:T(8,128)(2,1)S(1)}, bf16[1024,3,1,128]{3,0,2,1:T(8,128)(2,1)}, u32[]{:S(2)}) copy-start(bf16[1024,3,1,128]{3,0,2,1:T(8,128)(2,1)} %param.15) | copy-start | bytes 2359300
  111.5 0.7 copy-start.12
  154.2 6.1 %collective-permute-start = (bf16[24,1024]{1,0:T(8,128)(2,1)S(1)}, bf16[24,1024]{1,0:T(8,128)(2,1)S(1)}, u32[]{:S(2)}, u32[]{:S(2)}) collective-permute-start(bf16[24,1024]{1,0:T(8,128)(2,1)S(1)} %get-tuple-element.48), channel_id=1, source_target_pairs={{4,0},{8,4},{12,8},{16,12},{20,16},{24,20},{28,24},{5,1},{9,5},{13... | collective-permute-start | bytes 147464 | tf_op jit(solution)/shard_map/ppermute | solution.py:17
  155.5 4.8 %collective-permute-start.1 = (bf16[24,1024]{1,0:T(8,128)(2,1)S(1)}, bf16[24,1024]{1,0:T(8,128)(2,1)S(1)}, u32[]{:S(2)}, u32[]{:S(2)}) collective-permute-start(bf16[24,1024]{1,0:T(8,128)(2,1)S(1)} %get-tuple-element.49), channel_id=1, source_target_pairs={{0,4},{4,8},{8,12},{12,16},{16,20},{20,24},{24,28},{1,5},{5,9},{9,... | collective-permute-start | bytes 147464 | tf_op jit(solution)/shard_map/ppermute | solution.py:17
Sparse Core Ops, SparseCore 0:
  10.7 44.1 all-gather.6
  56.7 29.7 all-gather.4
  111.6 41.2 reduce-scatter.1

commit v3 on v2

--- a/solution.py
+++ b/solution.py
@@ -1,8 +1,11 @@
+import functools
 import math
 
 import jax
 import jax.numpy as jnp
 from jax import lax
+from jax.experimental import pallas as pl
+from jax.experimental.pallas import tpu as pltpu
 from jax.sharding import PartitionSpec as P
 
 BLOCK = 128
@@ -22,6 +25,82 @@
     for offset in range(conv_weight.shape[0]):
         summed = summed + conv_weight[offset] * padded[offset : offset + length].astype(jnp.float32)
     return jax.nn.silu(summed).astype(jnp.bfloat16)
+
+
+def exchange_kernel(plan, *refs):
+    count = len(plan)
+    inputs, outputs, semaphores = refs[:count], refs[count : 2 * count], refs[2 * count :]
+    barrier = pltpu.get_barrier_semaphore()
+    partners = 0
+    for axis in sorted({axis for axis, _, _ in plan}):
+        size, me = lax.axis_size(axis), lax.axis_index(axis)
+        for step in range(1, size):
+            pl.semaphore_signal(
+                barrier,
+                inc=1,
+                device_id={axis: lax.rem(me + step, size)},
+                device_id_type=pl.DeviceIdType.MESH,
+            )
+            partners += 1
+    pl.semaphore_wait(barrier, partners)
+    local_copies, sent, awaited = [], [], []
+    for item, (axis, scatter, _) in enumerate(plan):
+        source, target = inputs[item], outputs[item]
+        send, receive, own = semaphores[3 * item : 3 * item + 3]
+        size, me = lax.axis_size(axis), lax.axis_index(axis)
+        for step in range(1, size):
+            there, origin = lax.rem(me + step, size), lax.rem(me + size - step, size)
+
+            def copy(landing):
+                return pltpu.make_async_remote_copy(
+                    src_ref=source.at[there] if scatter else source,
+                    dst_ref=target.at[landing],
+                    send_sem=send.at[step],
+                    recv_sem=receive.at[step],
+                    device_id={axis: there},
+                    device_id_type=pl.DeviceIdType.MESH,
+                )
+
+            outgoing = copy(me)
+            outgoing.start()
+            sent.append(outgoing)
+            awaited.append(copy(origin))
+        kept = pltpu.make_async_copy(
+            source.at[me] if scatter else source, target.at[me], own.at[0]
+        )
+        kept.start()
+        local_copies.append(kept)
+    for kept in local_copies:
+        kept.wait()
+    for arriving in awaited:
+        arriving.wait_recv()
+    for outgoing in sent:
+        outgoing.wait_send()
+
+
+def exchange(number, *items):
+    plan = tuple((axis, scatter, array.shape) for array, axis, scatter in items)
+    scratch, shapes = [], []
+    for array, axis, scatter in items:
+        size = lax.axis_size(axis)
+        shapes.append(
+            jax.ShapeDtypeStruct(array.shape if scatter else (size, *array.shape), array.dtype)
+        )
+        scratch += [
+            pltpu.SemaphoreType.DMA((size,)),
+            pltpu.SemaphoreType.DMA((size,)),
+            pltpu.SemaphoreType.DMA((1,)),
+        ]
+    return pl.pallas_call(
+        functools.partial(exchange_kernel, plan),
+        out_shape=shapes,
+        in_specs=[pl.BlockSpec(memory_space=pltpu.VMEM)] * len(items),
+        out_specs=[pl.BlockSpec(memory_space=pltpu.VMEM)] * len(items),
+        scratch_shapes=scratch,
+        compiler_params=pltpu.CompilerParams(
+            collective_id=number, has_side_effects=True, vmem_limit_bytes=32 * 2**20
+        ),
+    )(*[array for array, _, _ in items])
 
 
 def pieces(values):
@@ -100,12 +179,10 @@
         ],
         axis=1,
     )
-    weight = lax.all_gather(weight, "head", axis=0, tiled=True)
+    to_gather = [(weight, "head", False)]
     if spread_out:
         here = [place + seq_count * k for k in range(shard_heads // seq_count)]
-        back = lax.all_gather(
-            head_columns(out_weight, 0, here, head_dim, 0), "head", axis=0, tiled=True
-        )
+        to_gather.append((head_columns(out_weight, 0, here, head_dim, 0), "head", False))
     else:
         rows = heads * head_dim
         owner = (place * rows) // out_weight.shape[0]
@@ -116,9 +193,13 @@
         float_states
         * lax.rsqrt(jnp.mean(float_states * float_states, axis=-1, keepdims=True) + 1e-05)
     ).astype(jnp.bfloat16)
-    gathered = lax.all_gather(
-        jnp.concatenate([normed, *pieces(decays)], axis=1), "seq", axis=0, tiled=True
-    )
+    unused = jnp.zeros((row_count, -3 * head_count % 128), jnp.bfloat16)
+    packed = jnp.concatenate([normed, *pieces(decays), unused], axis=1)
+    weight, *rest, gathered = exchange(0, *to_gather, (packed, "seq", False))
+    weight = weight.reshape(model_width, weight.shape[2])
+    if spread_out:
+        back = rest[0].reshape(heads * head_dim, model_width)
+    gathered = gathered.reshape(seq_count * row_count, packed.shape[1])
     length = gathered.shape[0]
     projected = jnp.dot(
         gathered[:, :model_width], weight, preferred_element_type=jnp.float32
@@ -159,8 +240,9 @@
     ).astype(jnp.bfloat16)
     flat = scaled.transpose(0, 2, 1, 3).reshape(length, width)
     share = jnp.dot(flat, back, preferred_element_type=jnp.float32).astype(jnp.bfloat16)
-    branch = lax.psum_scatter(share, "seq", scatter_dimension=0, tiled=True)
-    return (float_states + branch.astype(jnp.float32)).astype(jnp.bfloat16)
+    [shares] = exchange(1, (share.reshape(seq_count, row_count, model_width), "seq", True))
+    branch = jnp.sum(shares.astype(jnp.float32), axis=0)
+    return (float_states + branch).astype(jnp.bfloat16)
 
 
 def local(
@@ -196,20 +278,23 @@
     ).astype(jnp.bfloat16)
     key_width = qkv_weight.shape[3]
     projection = qkv_weight.reshape(model_width, 3 * key_width)
+    padded_groups = jnp.pad(group_normed, ((0, -per_device % 16), (0, 0)))
+    [every_group] = exchange(2, (padded_groups, "head", False))
     triple = jnp.dot(
-        lax.all_gather(group_normed, "head", axis=0, tiled=True),
+        every_group[:, :per_device].reshape(-1, model_width),
         projection,
         preferred_element_type=jnp.float32,
     ).astype(jnp.bfloat16)
     batch_rows = lax.axis_size("head")
     triple = triple.reshape(batch_rows, per_device, 3, key_width)
     query_rows = triple[:, :, 0]
-    key_rows = triple[:, :, 1]
-    values = triple[:, :, 2]
     query_pos = seq_index * per_device + jnp.arange(per_device, dtype=jnp.int32)
     row_max = jnp.full((batch_rows, per_device), -1e30, jnp.float32)
-    key_fragment = lax.all_gather(key_rows, "seq", axis=1, tiled=True)
-    value_piece = lax.all_gather(values, "seq", axis=1, tiled=True)
+    both = triple[:, :, 1:].reshape(batch_rows * per_device, 2 * key_width)
+    [both] = exchange(3, (jnp.pad(both, ((0, -both.shape[0] % 16), (0, 0))), "seq", False))
+    both = both[:, : batch_rows * per_device].reshape(seq_count, batch_rows, per_device, 2, key_width)
+    both = both.transpose(3, 1, 0, 2, 4).reshape(2, batch_rows, groups, key_width)
+    key_fragment, value_piece = both[0], both[1]
     key_count = key_fragment.shape[1]
     scores = jnp.einsum(
         "tfv,tuv->tfu", query_rows, key_fragment, preferred_element_type=jnp.float32

time: 204 us -> 138 us (0.68)
  Pallas kernels: 0 us -> 94.9 us
  waiting for transfers between devices: 88.9 us -> 0.69 us
  blocking collectives: 58.4 us -> 0 us
  between operations: 14.2 us -> 1.13 us
  matrix products: 11.8 us -> 6.53 us
  local copies, waits for them, and re-layouts: 17.6 us -> 20.3 us
    pallas_call x0 -> x4, Pallas kernels: none -> 94.9 us  [exchange(): pl.pallas_call(functools.partial(exchange_kernel, plan), out_shape=shapes...]
    all_gather x4 -> x0, blocking collectives: 58.4 us -> none  [the longest x1 24.2 us: encode(): lax.all_gather(head_columns(out_weight, 0, here, head_dim, 0), 'head', ax...]
    all_gather x2 -> x0, waiting for transfers between devices: 48.3 us -> none  [the longest x1 31.6 us: encode(): lax.all_gather(jnp.concatenate([normed, *pieces(decays)], axis=1), 'seq',...]
    reduce_scatter x1 -> x0, waiting for transfers between devices: 40.5 us -> none  [encode(): branch = lax.psum_scatter(share, 'seq', scatter_dimension=0, tiled=True)]
    unnamed x31 -> x27, local copies, waits for them, and re-layouts: 2.8 us -> 6.35 us
  transfers between devices with their start and end apart: 5 -> 2, of which waited for: 3 -> 1; matrix products, arithmetic and copies ran while one was open for 3% -> 1% of each run, Pallas kernels for 0% -> 0%
where the time goes in v3:
time: 138 us; the launch traced here: 137 us
  Pallas kernels  94.9 us (69%)
  local copies, waits for them, and re-layouts  20.3 us (15%)
  other arithmetic  9.2 us (7%)
  matrix products  6.53 us (5%)
  starting transfers between devices  4.48 us (3%)
    pallas_call x4, Pallas kernels, exchange(): pl.pallas_call(functools.partial(exchange_kernel, plan), out_shape=shapes...  94.9 us
    unnamed x27, local copies, waits for them, and re-layouts  6.35 us
    ppermute x2, starting transfers between devices, passed_along(): lax.ppermute(value, axis, [(source, source + steps) for source in range(f...  4.48 us
    dynamic_slice x6, local copies, waits for them, and re-layouts, head_columns(): lax.dynamic_slice_in_dim(array, first + head * head_dim, head_dim, axis)  4.32 us
    convert_element_type x2, local copies, waits for them, and re-layouts, encode(): gated = mixed * jax.nn.silu(gate.astype(jnp.float32))  4.14 us
  transfers between devices with their start and end apart: 2, of which 1 were waited for; matrix products, arithmetic and copies ran while one was open for 1% of the time, Pallas kernels for 0%

profile of v3, /device:TPU:0, one launch (start us, length us, event | category | flops | bytes accessed | tf_op | source)
XLA Modules:
  0.0 137.3 jit_solution(16817294237063144855)
XLA Ops:
  1.3 1.1 fusion.27
  2.4 1.1 fusion.28
  3.5 0.8 copy.67
  4.5 1.3 constant_dynamic-slice_fusion.5
  6.0 50.6 %shard_map.95 = (bf16[4,256,768]{2,1,0:T(8,128)(2,1)S(1)}, bf16[4,64,1024]{2,1,0:T(8,128)(2,1)S(1)}, bf16[8,128,1152]{2,1,0:T(8,128)(2,1)S(1)}) custom-call(bf16[256,768]{1,0:T(8,128)(2,1)S(1)} %concatenate.51.refs_0_, bf16[64,1024]{1,0:T(8,128)(2,1)S(1)} %constant_dynamic-slice_fusion.4.refs_1_, bf16[128,1152]{1,0:T(8,128)(2,1)S(1)} %concatenate.52.refs_2_), custom_call_target="tpu_custom_call" | custom-call | tf_op jit(solution)/shard_map/pallas_call | solution.py:94
  56.6 1.8 %fusion.2 = bf16[1024,768]{1,0:T(8,128)(2,1)S(1)} fusion(bf16[1024,768]{1,0:T(8,128)(2,1)S(1)} %bitcast.150, bf16[1024,1152]{1,0:T(8,128)(2,1)S(1)} %bitcast.147), kind=kOutput, calls=%fused_computation.6 | convolution fusion | flops 1611399168 | bytes 5242880 | tf_op jit(solution)/shard_map/dot_general | solution.py:204
  58.4 1.2 copy-done.6
  60.5 1.3 multiply_convert_fusion.1
  63.0 1.5 %fusion.91 = (bf16[1024,32]{1,0:T(8,128)(2,1)S(1)}, bf16[1024,32]{1,0:T(8,128)(2,1)S(1)}, bf16[1024,32]{1,0:T(8,128)(2,1)S(1)}) fusion(bf16[1024,1152]{1,0:T(8,128)(2,1)} %bitcast.148), kind=kLoop, calls=%fused_computation.174 | loop fusion | bytes 393216 | tf_op jit(solution)/shard_map/slice | solution.py:209
  65.2 1.3 dynamic-slice_reduce_fusion.3
  67.1 1.1 slice_convert_fusion
  68.3 1.0 copy.73
  69.3 1.9 %copy.120 = bf16[32,8,8,128]{3,2,1,0:T(8,128)(2,1)} copy(bf16[32,8,8,128]{3,1,2,0:T(8,128)(2,1)} %bitcast.159) | data formatting | bytes 1048576
  71.3 2.2 %reshape.219 = f32[8,128,4,64]{3,2,1,0:T(4,128)} reshape(f32[1024,256]{1,0:T(8,128)S(1)} %slice_convert_fusion) | data formatting | bytes 2097152 | tf_op jit(solution)/shard_map/convert_element_type | solution.py:236
  73.5 1.9 %copy.79 = f32[8,128,4,64]{1,3,2,0:T(8,128)S(1)} copy(f32[8,128,4,64]{3,2,1,0:T(4,128)} %reshape.219) | data formatting | bytes 2097152 | tf_op jit(solution)/shard_map/convert_element_type | solution.py:236
  75.4 0.9 fusion.95
  76.5 1.2 multiply_convert_fusion.3
  79.4 1.2 fusion.22
  82.3 24.4 %shard_map.96 = bf16[8,128,1024]{2,1,0:T(8,128)(2,1)S(1)} custom-call(bf16[8,128,1024]{2,1,0:T(8,128)(2,1)S(1)} %bitcast.145), custom_call_target="tpu_custom_call" | custom-call | tf_op jit(solution)/shard_map/pallas_call | solution.py:94
  108.0 3.2 %collective-permute-start.1 = (bf16[24,1024]{1,0:T(8,128)(2,1)S(1)}, bf16[24,1024]{1,0:T(8,128)(2,1)S(1)}, u32[]{:S(2)}, u32[]{:S(2)}) collective-permute-start(bf16[24,1024]{1,0:T(8,128)(2,1)S(1)} %get-tuple-element.57), channel_id=1, source_target_pairs={{0,4},{4,8},{8,12},{12,16},{16,20},{20,24},{24,28},{1,5},{5,9},{9,... | collective-permute-start | bytes 147464 | tf_op jit(solution)/shard_map/ppermute | solution.py:20
  111.2 1.3 collective-permute-start
  114.5 9.9 %shard_map.97 = bf16[4,32,1024]{2,1,0:T(8,128)(2,1)S(1)} custom-call(bf16[32,1024]{1,0:T(8,128)(2,1)S(1)} %pad.5.refs_0_), custom_call_target="tpu_custom_call" | custom-call | tf_op jit(solution)/shard_map/pallas_call | solution.py:94
  125.0 10.0 %shard_map.98 = bf16[8,96,256]{2,1,0:T(8,128)(2,1)S(1)} custom-call(bf16[96,256]{1,0:T(8,128)(2,1)S(1)} %bitcast.149), custom_call_target="tpu_custom_call" | custom-call | tf_op jit(solution)/shard_map/pallas_call | solution.py:94
  136.4 0.8 fusion.6
  (93 shorter events, 13.1 us)
Async XLA Ops:
  0.6 3.7 %copy-start = (bf16[512,1024]{1,0:T(8,128)(2,1)S(1)}, bf16[512,1024]{1,0:T(8,128)(2,1)}, u32[]{:S(2)}) copy-start(bf16[512,1024]{1,0:T(8,128)(2,1)} %param.14) | copy-start | bytes 3145732
  0.6 5.1 %slice-start.1 = ((bf16[256,4352]{1,0:T(8,128)(2,1)}), bf16[256,256]{1,0:T(8,128)(2,1)S(1)}, s32[]{:S(2)}) async-start(bf16[256,4352]{1,0:T(8,128)(2,1)} %param.11), calls=%async_computation.1 | async-start | bytes 262144 | tf_op jit(solution)/shard_map/slice | solution.py:178
  56.6 1.8 %copy-start.1 = (bf16[8,128,1152]{2,1,0:T(8,128)(2,1)}, bf16[8,128,1152]{2,1,0:T(8,128)(2,1)S(1)}, u32[]{:S(2)}) copy-start(bf16[8,128,1152]{2,1,0:T(8,128)(2,1)S(1)} %get-tuple-element.5) | copy-start | bytes 7077892
  58.4 1.2 copy-start.6
  59.6 0.8 copy-start.9
  59.6 0.8 slice-start.2
  61.9 1.1 copy-start.2
  65.2 3.1 %slice-start = ((bf16[1024,512]{1,0:T(8,128)(2,1)}), bf16[1024,256]{1,0:T(8,128)(2,1)S(1)}, s32[]{:S(2)}) async-start(bf16[1024,512]{1,0:T(8,128)(2,1)} %copy-done.2), calls=%async_computation | async-start | bytes 1048576 | tf_op jit(solution)/shard_map/slice | solution.py:230
  73.5 4.2 %copy-start.4 = (bf16[1024,128]{1,0:T(8,128)(2,1)S(1)}, bf16[1024,128]{1,0:T(8,128)(2,1)}, u32[]{:S(2)}) copy-start(bf16[1024,128]{1,0:T(8,128)(2,1)} %get-tuple-element.53) | copy-start | bytes 786436
  76.5 1.5 %copy-start.8 = (bf16[8,4,64,128]{3,2,1,0:T(8,128)(2,1)S(1)}, bf16[8,4,64,128]{3,2,1,0:T(8,128)(2,1)}, u32[]{:S(2)}) copy-start(bf16[8,4,64,128]{3,2,1,0:T(8,128)(2,1)} %broadcast_dynamic-update-slice_fusion) | copy-start | bytes 1572868
  78.4 1.0 copy-start.5
  106.7 0.7 copy-start.10
  106.7 1.0 copy-start.3
  106.7 6.6 %copy-start.7 = (bf16[1024,3,1,128]{3,0,2,1:T(8,128)(2,1)S(1)}, bf16[1024,3,1,128]{3,0,2,1:T(8,128)(2,1)}, u32[]{:S(2)}) copy-start(bf16[1024,3,1,128]{3,0,2,1:T(8,128)(2,1)} %param.15) | copy-start | bytes 2359300
  108.0 5.6 %collective-permute-start.1 = (bf16[24,1024]{1,0:T(8,128)(2,1)S(1)}, bf16[24,1024]{1,0:T(8,128)(2,1)S(1)}, u32[]{:S(2)}, u32[]{:S(2)}) collective-permute-start(bf16[24,1024]{1,0:T(8,128)(2,1)S(1)} %get-tuple-element.57), channel_id=1, source_target_pairs={{0,4},{4,8},{8,12},{12,16},{16,20},{20,24},{24,28},{1,5},{5,9},{9,... | collective-permute-start | bytes 147464 | tf_op jit(solution)/shard_map/ppermute | solution.py:20
  111.2 3.1 %collective-permute-start = (bf16[24,1024]{1,0:T(8,128)(2,1)S(1)}, bf16[24,1024]{1,0:T(8,128)(2,1)S(1)}, u32[]{:S(2)}, u32[]{:S(2)}) collective-permute-start(bf16[24,1024]{1,0:T(8,128)(2,1)S(1)} %get-tuple-element.56), channel_id=1, source_target_pairs={{4,0},{8,4},{12,8},{16,12},{20,16},{24,20},{28,24},{5,1},{9,5},{13... | collective-permute-start | bytes 147464 | tf_op jit(solution)/shard_map/ppermute | solution.py:20

commit v4 on v3

--- a/solution.py
+++ b/solution.py
@@ -25,6 +25,98 @@
     for offset in range(conv_weight.shape[0]):
         summed = summed + conv_weight[offset] * padded[offset : offset + length].astype(jnp.float32)
     return jax.nn.silu(summed).astype(jnp.bfloat16)
+
+
+def relay_step(axis, source, target, send, receive, step, finish=False):
+    size, me = lax.axis_size(axis), lax.axis_index(axis)
+    for lane, way in enumerate((1, -1)):
+        block = jnp.clip(me - way * step, 0, size - 1)
+        exists = (me >= step) if way == 1 else (me + step < size)
+        onward = (me + 1 < size) if way == 1 else (me >= 1)
+        copy = pltpu.make_async_remote_copy(
+            src_ref=source if step == 0 else target.at[block],
+            dst_ref=target.at[block],
+            send_sem=send.at[lane * size + step],
+            recv_sem=receive.at[block],
+            device_id={axis: jnp.clip(me + way, 0, size - 1)},
+            device_id_type=pl.DeviceIdType.MESH,
+        )
+        if finish:
+            pl.when(exists & onward)(copy.wait_send)
+            continue
+        if step:
+            pl.when(exists)(copy.wait_recv)
+        if step < size - 1:
+            pl.when(exists & onward)(copy.start)
+
+
+def pair_sum_kernel(
+    share, total, landed, summed, pair_send, pair_receive, far_send, far_receive
+):
+    size, me = lax.axis_size("seq"), lax.axis_index("seq")
+    pairs = size // 2
+    pair, side = me // 2, lax.rem(me, 2)
+    partner = 2 * pair + 1 - side
+    barrier = pltpu.get_barrier_semaphore()
+    peers = [partner] + [2 * lax.rem(pair + step, pairs) + side for step in range(1, pairs)]
+    for peer in peers:
+        pl.semaphore_signal(
+            barrier, inc=1, device_id={"seq": peer}, device_id_type=pl.DeviceIdType.MESH
+        )
+    pl.semaphore_wait(barrier, len(peers))
+    order = [*range(1, pairs), 0]
+    near = []
+    for step in order:
+        there = lax.rem(pair + step, pairs)
+        copy = pltpu.make_async_remote_copy(
+            src_ref=share.at[2 * there + 1 - side],
+            dst_ref=landed.at[step],
+            send_sem=pair_send.at[step],
+            recv_sem=pair_receive.at[step],
+            device_id={"seq": partner},
+            device_id_type=pl.DeviceIdType.MESH,
+        )
+        copy.start()
+        near.append(copy)
+    far = []
+    for step, arriving in zip(order, near):
+        there = lax.rem(pair + step, pairs)
+        arriving.wait_recv()
+        both = share[2 * there + side].astype(jnp.float32) + landed[step].astype(jnp.float32)
+        if step == 0:
+            total[0] = both.astype(jnp.bfloat16)
+            continue
+        summed[step] = both.astype(jnp.bfloat16)
+        copy = pltpu.make_async_remote_copy(
+            src_ref=summed.at[step],
+            dst_ref=total.at[step],
+            send_sem=far_send.at[step],
+            recv_sem=far_receive.at[step],
+            device_id={"seq": 2 * there + side},
+            device_id_type=pl.DeviceIdType.MESH,
+        )
+        copy.start()
+        far.append(copy)
+    for copy in far:
+        copy.wait_recv()
+    for copy in near + far:
+        copy.wait_send()
+
+
+def pair_sums(number, share):
+    pairs = share.shape[0] // 2
+    block = (pairs, *share.shape[1:])
+    return pl.pallas_call(
+        pair_sum_kernel,
+        out_shape=jax.ShapeDtypeStruct(block, share.dtype),
+        in_specs=[pl.BlockSpec(memory_space=pltpu.VMEM)],
+        out_specs=pl.BlockSpec(memory_space=pltpu.VMEM),
+        scratch_shapes=[pltpu.VMEM(block, share.dtype)] * 2
+        + [pltpu.SemaphoreType.DMA((pairs,))] * 4,
+        compiler_params=pltpu.CompilerParams(
+            collective_id=number, has_side_effects=True, vmem_limit_bytes=40 * 2**20
+        ),
+    )(share)
 
 
 def exchange_kernel(plan, *refs):
@@ -43,11 +135,19 @@
             )
             partners += 1
     pl.semaphore_wait(barrier, partners)
-    local_copies, sent, awaited = [], [], []
-    for item, (axis, scatter, _) in enumerate(plan):
+    local_copies, sent, awaited, relays = [], [], [], []
+    for item, (axis, scatter, relayed) in enumerate(plan):
         source, target = inputs[item], outputs[item]
         send, receive, own = semaphores[3 * item : 3 * item + 3]
         size, me = lax.axis_size(axis), lax.axis_index(axis)
+        if relayed:
+            relay = functools.partial(relay_step, axis, source, target, send, receive)
+            relay(0)
+            relays.append((relay, size))
+            kept = pltpu.make_async_copy(source, target.at[me], own.at[0])
+            kept.start()
+            local_copies.append(kept)
+            continue
         for step in range(1, size):
             there, origin = lax.rem(me + step, size), lax.rem(me + size - step, size)
 
@@ -70,6 +170,13 @@
         )
         kept.start()
         local_copies.append(kept)
+    for step in range(1, max([size for _, size in relays], default=0)):
+        for relay, size in relays:
+            if step < size:
+                relay(step)
+    for relay, size in relays:
+        for step in range(size - 1):
+            relay(step, finish=True)
     for kept in local_copies:
         kept.wait()
     for arriving in awaited:
@@ -79,15 +186,17 @@
 
 
 def exchange(number, *items):
-    plan = tuple((axis, scatter, array.shape) for array, axis, scatter in items)
+    plan = tuple((axis, kind == "scatter", kind == "relay") for _, axis, kind in items)
     scratch, shapes = [], []
-    for array, axis, scatter in items:
+    for array, axis, kind in items:
         size = lax.axis_size(axis)
         shapes.append(
-            jax.ShapeDtypeStruct(array.shape if scatter else (size, *array.shape), array.dtype)
+            jax.ShapeDtypeStruct(
+                array.shape if kind == "scatter" else (size, *array.shape), array.dtype
+            )
         )
         scratch += [
-            pltpu.SemaphoreType.DMA((size,)),
+            pltpu.SemaphoreType.DMA((2 * size,)),
             pltpu.SemaphoreType.DMA((size,)),
             pltpu.SemaphoreType.DMA((1,)),
         ]
@@ -179,10 +288,10 @@
         ],
         axis=1,
     )
-    to_gather = [(weight, "head", False)]
+    to_gather = [(weight, "head", "relay")]
     if spread_out:
         here = [place + seq_count * k for k in range(shard_heads // seq_count)]
-        to_gather.append((head_columns(out_weight, 0, here, head_dim, 0), "head", False))
+        to_gather.append((head_columns(out_weight, 0, here, head_dim, 0), "head", "relay"))
     else:
         rows = heads * head_dim
         owner = (place * rows) // out_weight.shape[0]
@@ -195,7 +304,7 @@
     ).astype(jnp.bfloat16)
     unused = jnp.zeros((row_count, -3 * head_count % 128), jnp.bfloat16)
     packed = jnp.concatenate([normed, *pieces(decays), unused], axis=1)
-    weight, *rest, gathered = exchange(0, *to_gather, (packed, "seq", False))
+    weight, *rest, gathered = exchange(0, *to_gather, (packed, "seq", "gather"))
     weight = weight.reshape(model_width, weight.shape[2])
     if spread_out:
         back = rest[0].reshape(heads * head_dim, model_width)
@@ -240,7 +349,7 @@
     ).astype(jnp.bfloat16)
     flat = scaled.transpose(0, 2, 1, 3).reshape(length, width)
     share = jnp.dot(flat, back, preferred_element_type=jnp.float32).astype(jnp.bfloat16)
-    [shares] = exchange(1, (share.reshape(seq_count, row_count, model_width), "seq", True))
+    shares = pair_sums(1, share.reshape(seq_count, row_count, model_width))
     branch = jnp.sum(shares.astype(jnp.float32), axis=0)
     return (float_states + branch).astype(jnp.bfloat16)
 
@@ -279,7 +388,7 @@
     key_width = qkv_weight.shape[3]
     projection = qkv_weight.reshape(model_width, 3 * key_width)
     padded_groups = jnp.pad(group_normed, ((0, -per_device % 16), (0, 0)))
-    [every_group] = exchange(2, (padded_groups, "head", False))
+    [every_group] = exchange(2, (padded_groups, "head", "gather"))
     triple = jnp.dot(
         every_group[:, :per_device].reshape(-1, model_width),
         projection,
@@ -291,7 +400,7 @@
     query_pos = seq_index * per_device + jnp.arange(per_device, dtype=jnp.int32)
     row_max = jnp.full((batch_rows, per_device), -1e30, jnp.float32)
     both = triple[:, :, 1:].reshape(batch_rows * per_device, 2 * key_width)
-    [both] = exchange(3, (jnp.pad(both, ((0, -both.shape[0] % 16), (0, 0))), "seq", False))
+    [both] = exchange(3, (jnp.pad(both, ((0, -both.shape[0] % 16), (0, 0))), "seq", "gather"))
     both = both[:, : batch_rows * per_device].reshape(seq_count, batch_rows, per_device, 2, key_width)
     both = both.transpose(3, 1, 0, 2, 4).reshape(2, batch_rows, groups, key_width)
     key_fragment, value_piece = both[0], both[1]

time: 138 us -> 117 us (0.85)
  Pallas kernels: 94.9 us -> 74.6 us
    pallas_call x4 -> x3, Pallas kernels: 94.9 us -> 59.3 us  [exchange(): pl.pallas_call(functools.partial(exchange_kernel, plan), out_shape=shapes...]
    pallas_call x0 -> x1, Pallas kernels: none -> 15.3 us  [pair_sums(): pl.pallas_call(pair_sum_kernel, out_shape=jax.ShapeDtypeStruct(block, sha...]
where the time goes in v4:
time: 117 us
  Pallas kernels  74.6 us (64%)
  local copies, waits for them, and re-layouts  19.9 us (17%)
  other arithmetic  9.04 us (8%)
  matrix products  6.54 us (6%)
  starting transfers between devices  3.65 us (3%)
  waiting for transfers between devices  1.67 us (1%)
    pallas_call x3, Pallas kernels, exchange(): pl.pallas_call(functools.partial(exchange_kernel, plan), out_shape=shapes...  59.3 us
    pallas_call x1, Pallas kernels, pair_sums(): pl.pallas_call(pair_sum_kernel, out_shape=jax.ShapeDtypeStruct(block, sha...  15.3 us
    unnamed x27, local copies, waits for them, and re-layouts  5.91 us
    dynamic_slice x6, local copies, waits for them, and re-layouts, head_columns(): lax.dynamic_slice_in_dim(array, first + head * head_dim, head_dim, axis)  4.32 us
    convert_element_type x2, local copies, waits for them, and re-layouts, encode(): gated = mixed * jax.nn.silu(gate.astype(jnp.float32))  4.14 us
    ppermute x2, starting transfers between devices, passed_along(): lax.ppermute(value, axis, [(source, source + steps) for source in range(f...  3.65 us
  transfers between devices with their start and end apart: 2, of which 1 were waited for; matrix products, arithmetic and copies ran while one was open for 1% of the time, Pallas kernels for 0%

profile of v4, /device:TPU:0, one launch (start us, length us, event | category | flops | bytes accessed | tf_op | source)
XLA Modules:
  0.0 116.5 jit_solution(3829487151804001009)
XLA Ops:
  1.3 1.1 fusion.27
  2.4 1.1 fusion.28
  4.5 1.3 %constant_dynamic-slice_fusion.5 = (bf16[256,64]{1,0:T(8,128)(2,1)S(1)}, bf16[256,64]{1,0:T(8,128)(2,1)S(1)}, bf16[256,64]{1,0:T(8,128)(2,1)S(1)}, bf16[256,64]{...) fusion(bf16[256,4352]{1,0:T(8,128)(2,1)} %param.11, ...), kind=kLoop, calls=%fused_computation.140 | loop fusion | bytes 524320 | tf_op jit(solution)/shard_map/dynamic_slice | solution.py:227
  6.0 40.7 %shard_map.95 = (bf16[4,256,768]{2,1,0:T(8,128)(2,1)S(1)}, bf16[4,64,1024]{2,1,0:T(8,128)(2,1)S(1)}, bf16[8,128,1152]{2,1,0:T(8,128)(2,1)S(1)}) custom-call(bf16[256,768]{1,0:T(8,128)(2,1)S(1)} %concatenate.51.refs_0_, bf16[64,1024]{1,0:T(8,128)(2,1)S(1)} %constant_dynamic-slice_fusion.4.refs_1_, bf16[128,1152]{1,0:T(8,128)(2,1)S(1)} %concatenate.52.refs_2_), custom_call_target="tpu_custom_call" | custom-call | tf_op jit(solution)/shard_map/pallas_call | solution.py:203
  46.8 1.8 %fusion.2 = bf16[1024,768]{1,0:T(8,128)(2,1)S(1)} fusion(bf16[1024,768]{1,0:T(8,128)(2,1)S(1)} %bitcast.150, bf16[1024,1152]{1,0:T(8,128)(2,1)S(1)} %bitcast.147), kind=kOutput, calls=%fused_computation.6 | convolution fusion | flops 1611399168 | bytes 5242880 | tf_op jit(solution)/shard_map/dot_general | solution.py:313
  48.6 1.2 copy-done.6
  50.7 1.3 %multiply_convert_fusion.1 = bf16[1024,512]{1,0:T(8,128)(2,1)S(1)} fusion(bf16[1024,512]{1,0:T(8,128)(2,1)S(1)} %slice.187, f32[512]{0:T(512)S(1)} %bitcast.166, f32[512]{0:T(512)S(1)} %bitcast.167, f32[512]{0:T(512)S(1)} %bitcast.168, f32[512]{0:T(512)S(1)} %bitcast.165), kind=kLoop, calls=%fused_computation.4 | loop fusion | flops 8388608 | bytes 2105344 | tf_op jit(solution)/shard_map/convert_element_type | solution.py:27
  53.1 1.5 %fusion.91 = (bf16[1024,32]{1,0:T(8,128)(2,1)S(1)}, bf16[1024,32]{1,0:T(8,128)(2,1)S(1)}, bf16[1024,32]{1,0:T(8,128)(2,1)S(1)}) fusion(bf16[1024,1152]{1,0:T(8,128)(2,1)} %bitcast.148), kind=kLoop, calls=%fused_computation.174 | loop fusion | bytes 393216 | tf_op jit(solution)/shard_map/slice | solution.py:318
  55.3 1.3 %dynamic-slice_reduce_fusion.3 = (bf16[1024]{0:T(1024)(128)(2,1)S(1)}, bf16[1024]{0:T(1024)(128)(2,1)S(1)}, bf16[1024]{0:T(1024)(128)(2,1)S(1)}, bf16[1024]{0:T(...) fusion(bf16[1024,32]{1,0:T(8,128)(2,1)S(1)} %get-tuple-element., ...), kind=kLoop, calls=%fused_computation.54 | loop fusion | bytes 32784 | tf_op jit(solution)/shard_map/dynamic_slice | solution.py:227
  57.2 1.1 slice_convert_fusion
  58.4 1.0 copy.73
  59.4 1.9 %copy.120 = bf16[32,8,8,128]{3,2,1,0:T(8,128)(2,1)} copy(bf16[32,8,8,128]{3,1,2,0:T(8,128)(2,1)} %bitcast.159) | data formatting | bytes 1048576
  61.4 2.2 %reshape.219 = f32[8,128,4,64]{3,2,1,0:T(4,128)} reshape(f32[1024,256]{1,0:T(8,128)S(1)} %slice_convert_fusion) | data formatting | bytes 2097152 | tf_op jit(solution)/shard_map/convert_element_type | solution.py:345
  63.7 1.9 %copy.79 = f32[8,128,4,64]{1,3,2,0:T(8,128)S(1)} copy(f32[8,128,4,64]{3,2,1,0:T(4,128)} %reshape.219) | data formatting | bytes 2097152 | tf_op jit(solution)/shard_map/convert_element_type | solution.py:345
  65.6 0.9 fusion.95
  66.6 1.2 %multiply_convert_fusion.3 = bf16[8,128,4,64]{1,0,3,2:T(8,128)(2,1)S(1)} fusion(bf16[8,128,4,64]{1,0,3,2:T(8,128)(2,1)} %bitcast.157, f32[8,128,4]{1,0,2:T(8,128)S(1)} %get-tuple-element.66), kind=kLoop, calls=%fused_computation.27 | loop fusion | flops 786432 | bytes 1064960 | tf_op jit(solution)/shard_map/convert_element_type | solution.py:253
  69.6 1.2 %fusion.22 = (f32[8,4,128]{2,1,0:T(4,128)S(1)}, f32[8,4,128,64]{2,3,1,0:T(8,128)S(1)}) fusion(f32[8,128,4,64]{1,3,2,0:T(8,128)S(1)} %copy.79, f32[8,4,64,128]{3,2,1,0:T(8,128)S(1)} %fusion.99, f32[8,4,128]{2,1,0:T(4,128)S(1)} %copy.80, bf16[8,128,4,64]{1,0,3,2:T(8,128)(2,1)S(1)} %bitcast.158, f32[8,128,128]{2,1,0:T(8,128)S(1)} %fusion.98, ...), kind=kOutput, calls=%fused_computation.33 | convolution fusion | flops 72085504 | bytes 4259840 | tf_op jit(solution)/shard_map/bhts,bshp->bhtp/dot_general | solution.py:248
  72.4 15.3 %shard_map.96 = bf16[4,128,1024]{2,1,0:T(8,128)(2,1)S(1)} custom-call(bf16[8,128,1024]{2,1,0:T(8,128)(2,1)S(1)} %bitcast.145), custom_call_target="tpu_custom_call" | custom-call | tf_op jit(solution)/shard_map/pallas_call | solution.py:109
  88.5 2.4 %collective-permute-start.1 = (bf16[24,1024]{1,0:T(8,128)(2,1)S(1)}, bf16[24,1024]{1,0:T(8,128)(2,1)S(1)}, u32[]{:S(2)}, u32[]{:S(2)}) collective-permute-start(bf16[24,1024]{1,0:T(8,128)(2,1)S(1)} %get-tuple-element.57), channel_id=1, source_target_pairs={{0,4},{4,8},{8,12},{12,16},{16,20},{20,24},{24,28},{1,5},{5,9},{9,... | collective-permute-start | bytes 147464 | tf_op jit(solution)/shard_map/ppermute | solution.py:20
  90.8 1.3 %collective-permute-start = (bf16[24,1024]{1,0:T(8,128)(2,1)S(1)}, bf16[24,1024]{1,0:T(8,128)(2,1)S(1)}, u32[]{:S(2)}, u32[]{:S(2)}) collective-permute-start(bf16[24,1024]{1,0:T(8,128)(2,1)S(1)} %get-tuple-element.56), channel_id=1, source_target_pairs={{4,0},{8,4},{12,8},{16,12},{20,16},{24,20},{28,24},{5,1},{9,5},{13... | collective-permute-start | bytes 147464 | tf_op jit(solution)/shard_map/ppermute | solution.py:20
  93.3 1.7 %collective-permute-done = bf16[24,1024]{1,0:T(8,128)(2,1)S(1)} collective-permute-done((bf16[24,1024]{1,0:T(8,128)(2,1)S(1)}, bf16[24,1024]{1,0:T(8,128)(2,1)S(1)}, u32[]{:S(2)}, u32[]{:S(2)}) %collective-permute-start) | collective-permute-done | bytes 49184 | tf_op jit(solution)/shard_map/ppermute | solution.py:20
  95.2 6.4 %shard_map.97 = bf16[4,32,1024]{2,1,0:T(8,128)(2,1)S(1)} custom-call(bf16[32,1024]{1,0:T(8,128)(2,1)S(1)} %pad.5.refs_0_), custom_call_target="tpu_custom_call" | custom-call | tf_op jit(solution)/shard_map/pallas_call | solution.py:203
  102.1 12.2 %shard_map.98 = bf16[8,96,256]{2,1,0:T(8,128)(2,1)S(1)} custom-call(bf16[96,256]{1,0:T(8,128)(2,1)S(1)} %bitcast.149), custom_call_target="tpu_custom_call" | custom-call | tf_op jit(solution)/shard_map/pallas_call | solution.py:203
  115.7 0.8 fusion.6
  (93 shorter events, 12.6 us)
Async XLA Ops:
  0.6 3.7 %copy-start = (bf16[512,1024]{1,0:T(8,128)(2,1)S(1)}, bf16[512,1024]{1,0:T(8,128)(2,1)}, u32[]{:S(2)}) copy-start(bf16[512,1024]{1,0:T(8,128)(2,1)} %param.14) | copy-start | bytes 3145732
  0.6 5.1 %slice-start.1 = ((bf16[256,4352]{1,0:T(8,128)(2,1)}), bf16[256,256]{1,0:T(8,128)(2,1)S(1)}, s32[]{:S(2)}) async-start(bf16[256,4352]{1,0:T(8,128)(2,1)} %param.11), calls=%async_computation.1 | async-start | bytes 262144 | tf_op jit(solution)/shard_map/slice | solution.py:287
  46.7 1.8 %copy-start.1 = (bf16[8,128,1152]{2,1,0:T(8,128)(2,1)}, bf16[8,128,1152]{2,1,0:T(8,128)(2,1)S(1)}, u32[]{:S(2)}) copy-start(bf16[8,128,1152]{2,1,0:T(8,128)(2,1)S(1)} %get-tuple-element.5) | copy-start | bytes 7077892
  48.6 1.2 copy-start.6
  49.7 0.8 copy-start.9
  49.7 0.8 slice-start.2
  52.0 1.1 copy-start.2
  55.3 3.1 %slice-start = ((bf16[1024,512]{1,0:T(8,128)(2,1)}), bf16[1024,256]{1,0:T(8,128)(2,1)S(1)}, s32[]{:S(2)}) async-start(bf16[1024,512]{1,0:T(8,128)(2,1)} %copy-done.2), calls=%async_computation | async-start | bytes 1048576 | tf_op jit(solution)/shard_map/slice | solution.py:339
  63.7 4.2 %copy-start.4 = (bf16[1024,128]{1,0:T(8,128)(2,1)S(1)}, bf16[1024,128]{1,0:T(8,128)(2,1)}, u32[]{:S(2)}) copy-start(bf16[1024,128]{1,0:T(8,128)(2,1)} %get-tuple-element.53) | copy-start | bytes 786436
  66.6 1.5 %copy-start.8 = (bf16[8,4,64,128]{3,2,1,0:T(8,128)(2,1)S(1)}, bf16[8,4,64,128]{3,2,1,0:T(8,128)(2,1)}, u32[]{:S(2)}) copy-start(bf16[8,4,64,128]{3,2,1,0:T(8,128)(2,1)} %broadcast_dynamic-update-slice_fusion) | copy-start | bytes 1572868
  68.5 1.0 copy-start.5
  72.4 15.6 %copy-start.10 = (s32[1,192]{1,0:T(1,128)S(1)}, s32[1,192]{1,0:T(1,128)}, u32[]{:S(2)}) copy-start(s32[1,192]{1,0:T(1,128)} %param.10) | copy-start | bytes 2308
  72.4 15.7 %copy-start.3 = (bf16[1,128,1024]{2,1,0:T(8,128)(2,1)S(1)}, bf16[1,128,1024]{2,1,0:T(8,128)(2,1)}, u32[]{:S(2)}) copy-start(bf16[1,128,1024]{2,1,0:T(8,128)(2,1)} %param.8) | copy-start | bytes 786436
  87.8 5.2 %copy-start.7 = (bf16[1024,3,1,128]{3,0,2,1:T(8,128)(2,1)S(1)}, bf16[1024,3,1,128]{3,0,2,1:T(8,128)(2,1)}, u32[]{:S(2)}) copy-start(bf16[1024,3,1,128]{3,0,2,1:T(8,128)(2,1)} %param.15) | copy-start | bytes 2359300
  88.5 4.8 %collective-permute-start.1 = (bf16[24,1024]{1,0:T(8,128)(2,1)S(1)}, bf16[24,1024]{1,0:T(8,128)(2,1)S(1)}, u32[]{:S(2)}, u32[]{:S(2)}) collective-permute-start(bf16[24,1024]{1,0:T(8,128)(2,1)S(1)} %get-tuple-element.57), channel_id=1, source_target_pairs={{0,4},{4,8},{8,12},{12,16},{16,20},{20,24},{24,28},{1,5},{5,9},{9,... | collective-permute-start | bytes 147464 | tf_op jit(solution)/shard_map/ppermute | solution.py:20
  90.8 4.1 %collective-permute-start = (bf16[24,1024]{1,0:T(8,128)(2,1)S(1)}, bf16[24,1024]{1,0:T(8,128)(2,1)S(1)}, u32[]{:S(2)}, u32[]{:S(2)}) collective-permute-start(bf16[24,1024]{1,0:T(8,128)(2,1)S(1)} %get-tuple-element.56), channel_id=1, source_target_pairs={{4,0},{8,4},{12,8},{16,12},{20,16},{24,20},{28,24},{5,1},{9,5},{13... | collective-permute-start | bytes 147464 | tf_op jit(solution)/shard_map/ppermute | solution.py:20

commit v5 on v4

--- a/solution.py
+++ b/solution.py
@@ -231,38 +231,85 @@
     )
 
 
-def mix(head_inputs, write_vectors, read_vectors, decays):
-    blocks, length, heads, head_dim = head_inputs.shape
+def mix_kernel(heads, convolved, gate, down, across, gain, back, share, state):
+    length = convolved.shape[0]
+    width = gate.shape[1]
+    head_dim = width // heads
+    state_width = (convolved.shape[1] - width) // 2
+
+    @pl.when(pl.program_id(0) == 0)
+    def _():
+        state[...] = jnp.zeros_like(state)
+
     later = lax.broadcasted_iota(jnp.int32, (length, length), 0)
     earlier = lax.broadcasted_iota(jnp.int32, (length, length), 1)
     causal = earlier <= later
-    cumulative = jnp.einsum(
-        "ts,bsh->bht", causal.astype(jnp.float32), decays, precision=highest
-    )
-    spread = cumulative[:, :, :, None] - cumulative[:, :, None, :]
-    factor = jnp.where(causal, jnp.exp(jnp.where(causal, spread, 0.0)), 0.0)
-    gram_matrix = jnp.einsum(
-        "btn,bsn->bts", read_vectors, write_vectors, preferred_element_type=jnp.float32
-    )
-    mixed = (factor * gram_matrix[:, None]).astype(jnp.bfloat16)
-    output = jnp.einsum("bhts,bshp->bhtp", mixed, head_inputs, preferred_element_type=jnp.float32)
-    final_log = cumulative[:, :, -1]
-    tail_decay = jnp.exp(final_log[:, :, None] - cumulative)
-    weighted = (
-        head_inputs.astype(jnp.float32) * tail_decay.transpose(0, 2, 1)[..., None]
-    ).astype(jnp.bfloat16)
-    fresh = jnp.einsum(
-        "bshp,bsn->bhpn", weighted, write_vectors, preferred_element_type=jnp.float32
-    )
-    state = jnp.zeros_like(fresh[0])
-    before = []
-    for block in range(blocks):
-        before.append(state.astype(jnp.bfloat16))
-        state = jnp.exp(final_log[block])[:, None, None] * state + fresh[block]
-    carried = jnp.einsum(
-        "btn,bhpn->bhtp", read_vectors, jnp.stack(before), preferred_element_type=jnp.float32
-    )
-    return output + jnp.exp(cumulative)[..., None] * carried
+    write_vectors = convolved[:, width : width + state_width]
+    read_vectors = convolved[:, width + state_width :]
+    along = (((1,), (1,)), ((), ()))
+    gram_matrix = lax.dot_general(
+        read_vectors, write_vectors, along, preferred_element_type=jnp.float32
+    )
+    done = []
+    for head in range(heads):
+        columns = slice(head * head_dim, (head + 1) * head_dim)
+        at_t, at_s = down[:, head : head + 1], across[0, head : head + 1, :]
+        factor = jnp.where(causal, jnp.exp(jnp.where(causal, at_t - at_s, 0.0)), 0.0)
+        mixed = (factor * gram_matrix).astype(jnp.bfloat16)
+        inputs = convolved[:, columns]
+        output = jnp.dot(mixed, inputs, preferred_element_type=jnp.float32)
+        before = state[head]
+        carried = lax.dot_general(
+            read_vectors, before.astype(jnp.bfloat16), along, preferred_element_type=jnp.float32
+        )
+        output = output + jnp.exp(at_t) * carried
+        last = at_t[length - 1 :]
+        weighted = (inputs.astype(jnp.float32) * jnp.exp(last - at_t)).astype(jnp.bfloat16)
+        fresh = lax.dot_general(
+            weighted, write_vectors, (((0,), (0,)), ((), ())), preferred_element_type=jnp.float32
+        )
+        state[head] = jnp.exp(last) * before + fresh
+        own_gate = gate[:, columns].astype(jnp.float32)
+        gated = output * (own_gate / (1.0 + jnp.exp(-own_gate)))
+        square = jnp.mean(gated * gated, axis=-1, keepdims=True)
+        done.append((gated * lax.rsqrt(square + 1e-05) * gain[:, columns]).astype(jnp.bfloat16))
+    flat = done[0] if heads == 1 else jnp.concatenate(done, axis=1)
+    share[...] = jnp.dot(flat, back[...], preferred_element_type=jnp.float32).astype(jnp.bfloat16)
+
+
+def mix(convolved, gate, decays, gain, back):
+    length, heads = decays.shape
+    blocks, width, model_width = length // BLOCK, gate.shape[1], back.shape[1]
+    state_width = (convolved.shape[1] - width) // 2
+    row = lax.broadcasted_iota(jnp.int32, (BLOCK, BLOCK), 0)
+    column = lax.broadcasted_iota(jnp.int32, (BLOCK, BLOCK), 1)
+    across = jnp.einsum(
+        "ts,bsh->bht",
+        (column <= row).astype(jnp.float32),
+        decays.reshape(blocks, BLOCK, heads),
+        precision=highest,
+    )
+    down = across.transpose(0, 2, 1).reshape(length, heads)
+
+    def rows(columns):
+        return pl.BlockSpec((BLOCK, columns), lambda i: (i, 0))
+
+    return pl.pallas_call(
+        functools.partial(mix_kernel, heads),
+        grid=(blocks,),
+        out_shape=jax.ShapeDtypeStruct((length, model_width), jnp.bfloat16),
+        in_specs=[
+            rows(convolved.shape[1]),
+            rows(width),
+            rows(heads),
+            pl.BlockSpec((1, heads, BLOCK), lambda i: (i, 0, 0)),
+            pl.BlockSpec((1, width), lambda i: (0, 0)),
+            pl.BlockSpec((width, model_width), lambda i: (0, 0)),
+        ],
+        out_specs=rows(model_width),
+        scratch_shapes=[pltpu.VMEM((heads, width // heads, state_width), jnp.float32)],
+        compiler_params=pltpu.CompilerParams(vmem_limit_bytes=16 * 2**20),
+    )(convolved, gate, down, across, gain, back)
 
 
 def encode(states, decays, in_weight, conv_weight, norm_gain, out_weight):
@@ -334,21 +381,8 @@
         [jnp.zeros((conv_weight.shape[0] - 1, mixer_in.shape[1]), jnp.bfloat16), mixer_in], axis=0
     )
     convolved = convolve(padded, taps, length)
-    blocks = length // BLOCK
-    mixed = mix(
-        convolved[:, :width].reshape(blocks, BLOCK, heads, head_dim),
-        convolved[:, width : width + state_width].reshape(blocks, BLOCK, state_width),
-        convolved[:, width + state_width :].reshape(blocks, BLOCK, state_width),
-        own_decays.reshape(blocks, BLOCK, heads),
-    )
-    gate = projected[:, :width].reshape(blocks, BLOCK, heads, head_dim).transpose(0, 2, 1, 3)
-    gated = mixed * jax.nn.silu(gate.astype(jnp.float32))
-    gain = head_columns(norm_gain, 0, own_heads, head_dim, 0).reshape(heads, 1, head_dim)
-    scaled = (
-        gated * lax.rsqrt(jnp.mean(gated * gated, axis=-1, keepdims=True) + 1e-05) * gain
-    ).astype(jnp.bfloat16)
-    flat = scaled.transpose(0, 2, 1, 3).reshape(length, width)
-    share = jnp.dot(flat, back, preferred_element_type=jnp.float32).astype(jnp.bfloat16)
+    gain = head_columns(norm_gain, 0, own_heads, head_dim, 0).reshape(1, width)
+    share = mix(convolved, projected[:, :width], own_decays, gain, back)
     shares = pair_sums(1, share.reshape(seq_count, row_count, model_width))
     branch = jnp.sum(shares.astype(jnp.float32), axis=0)
     return (float_states + branch).astype(jnp.bfloat16)

time: 117 us -> 111 us (0.949)
  local copies, waits for them, and re-layouts: 19.9 us -> 8.53 us
  Pallas kernels: 74.6 us -> 84.5 us
  matrix products: 6.54 us -> 3.73 us
    pallas_call x0 -> x1, Pallas kernels: none -> 9.93 us  [mix(): pl.pallas_call(functools.partial(mix_kernel, heads), grid=(blocks,), out_...]
    unnamed x27 -> x13, local copies, waits for them, and re-layouts: 5.91 us -> 1.14 us
    convert_element_type x3 -> x0, local copies, waits for them, and re-layouts: 4.49 us -> none  [the longest x2 4.14 us: encode(): gated = mixed * jax.nn.silu(gate.astype(jnp.float32))]
    convert_element_type x3 -> x0, other arithmetic: 2.84 us -> none  [the longest x1 1.21 us: mix(): weighted = (head_inputs.astype(jnp.float32) * tail_decay.transpose(0, 2,...]
    dot_general x6 -> x1, matrix products: 2.94 us -> 0.13 us  [mix(): jnp.einsum('ts,bsh->bht', (column <= row).astype(jnp.float32), decays.res...]
    convert_element_type x1, other arithmetic: 1.33 us -> 4.06 us  [convolve(): return jax.nn.silu(summed).astype(jnp.bfloat16)]
    slice x5 -> x1, local copies, waits for them, and re-layouts: 2.03 us -> 0.03 us  [encode(): share = mix(convolved, projected[:, :width], own_decays, gain, back)]
    slice x1, local copies, waits for them, and re-layouts: 1.48 us -> 0.21 us  [encode(): gathered[:, model_width + k * head_count:model_width + (k + 1) * head_count]]
where the time goes in v5:
time: 111 us
  Pallas kernels  84.5 us (76%)
  local copies, waits for them, and re-layouts  8.53 us (8%)
  other arithmetic  7.96 us (7%)
  matrix products  3.73 us (3%)
  starting transfers between devices  3.65 us (3%)
  waiting for transfers between devices  1.7 us (2%)
    pallas_call x3, Pallas kernels, exchange(): pl.pallas_call(functools.partial(exchange_kernel, plan), out_shape=shapes...  59.3 us
    pallas_call x1, Pallas kernels, pair_sums(): pl.pallas_call(pair_sum_kernel, out_shape=jax.ShapeDtypeStruct(block, sha...  15.4 us
    pallas_call x1, Pallas kernels, mix(): pl.pallas_call(functools.partial(mix_kernel, heads), grid=(blocks,), out_...  9.93 us
    dynamic_slice x6, local copies, waits for them, and re-layouts, head_columns(): lax.dynamic_slice_in_dim(array, first + head * head_dim, head_dim, axis)  4.32 us
    convert_element_type x1, other arithmetic, convolve(): return jax.nn.silu(summed).astype(jnp.bfloat16)  4.06 us
    ppermute x2, starting transfers between devices, passed_along(): lax.ppermute(value, axis, [(source, source + steps) for source in range(f...  3.65 us
  transfers between devices with their start and end apart: 2, of which 1 were waited for; matrix products, arithmetic and copies ran while one was open for 1% of the time, Pallas kernels for 0%

profile of v5, /device:TPU:0, one launch (start us, length us, event | category | flops | bytes accessed | tf_op | source)
XLA Modules:
  0.0 111.1 jit_solution(6586060990938945520)
XLA Ops:
  0.7 1.2 %fusion.10 = f32[128]{0:T(128)S(1)} fusion(bf16[1,128,1024]{2,1,0:T(8,128)(2,1)} %param.8), kind=kLoop, calls=%fused_computation.16 | loop fusion | flops 393088 | bytes 262656 | tf_op jit(solution)/shard_map/reduce_sum | solution.py:350
  1.9 1.1 fusion.11
  2.9 0.8 copy.39
  4.0 1.3 %constant_dynamic-slice_fusion.1 = (bf16[256,64]{1,0:T(8,128)(2,1)S(1)}, bf16[256,64]{1,0:T(8,128)(2,1)S(1)}, bf16[256,64]{1,0:T(8,128)(2,1)S(1)}, bf16[256,64]{...) fusion(bf16[256,4352]{1,0:T(8,128)(2,1)} %param.11, ...), kind=kLoop, calls=%fused_computation.86 | loop fusion | bytes 524320 | tf_op jit(solution)/shard_map/dynamic_slice | solution.py:227
  5.5 40.7 %shard_map.95 = (bf16[4,256,768]{2,1,0:T(8,128)(2,1)S(1)}, bf16[4,64,1024]{2,1,0:T(8,128)(2,1)S(1)}, bf16[8,128,1152]{2,1,0:T(8,128)(2,1)S(1)}) custom-call(bf16[256,768]{1,0:T(8,128)(2,1)S(1)} %concatenate.52.refs_0_, bf16[64,1024]{1,0:T(8,128)(2,1)S(1)} %constant_dynamic-slice_fusion.refs_1_, bf16[128,1152]{1,0:T(8,128)(2,1)S(1)} %concatenate.53.refs_2_), custom_call_target="tpu_custom_call" | custom-call | tf_op jit(solution)/shard_map/pallas_call | solution.py:203
  46.2 1.8 %fusion.2 = bf16[1024,768]{1,0:T(8,128)(2,1)S(1)} fusion(bf16[1024,768]{1,0:T(8,128)(2,1)S(1)} %bitcast.84, bf16[1024,1152]{1,0:T(8,128)(2,1)S(1)} %bitcast.80), kind=kOutput, calls=%fused_computation.4 | convolution fusion | flops 1611399168 | bytes 5242880 | tf_op jit(solution)/shard_map/dot_general | solution.py:360
  48.0 1.1 slice.98
  49.6 0.7 dynamic-slice_reduce_fusion.11
  50.3 1.3 %dynamic-slice_reduce_fusion.3 = (bf16[1024]{0:T(1024)(128)(2,1)S(1)}, bf16[1024]{0:T(1024)(128)(2,1)S(1)}, bf16[1024]{0:T(1024)(128)(2,1)S(1)}, bf16[1024]{0:T(...) fusion(bf16[1024,32]{1,0:T(8,128)(2,1)S(1)} %get-tuple-element., ...), kind=kLoop, calls=%fused_computation.24 | loop fusion | bytes 32784 | tf_op jit(solution)/shard_map/dynamic_slice | solution.py:227
  52.1 0.9 fusion.60
  53.0 4.1 %multiply_convert_fusion.convolved = bf16[1024,512]{1,0:T(8,128)(2,1)S(1)} fusion(bf16[1024,512]{1,0:T(8,128)(2,1)} %slice.98, f32[512]{0:T(512)S(1)} %bitcast.93, f32[512]{0:T(512)S(1)} %bitcast.94, f32[512]{0:T(512)S(1)} %bitcast.95, f32[512]{0:T(512)S(1)} %bitcast.92), kind=kLoop, calls=%fused_computation.3 | loop fusion | flops 8388608 | bytes 2105344 | tf_op jit(solution)/shard_map/convert_element_type | solution.py:27
  57.1 9.9 %shard_map.96 = bf16[1024,1024]{1,0:T(8,128)(2,1)S(1)} custom-call(bf16[1024,512]{1,0:T(8,128)(2,1)S(1)} %multiply_convert_fusion.convolved, bf16[1024,256]{1,0:T(8,128)(2,1)S(1)} %slice.102.gate, f32[1024,4]{1,0:T(8,128)S(1)} %bitcast.78, f32[8,4,128]{2,1,0:T(4,128)S(1)} %copy.44.across, f32[1,256]{1,0:T(1,128)S(1)} %bitcast.83, bf16[256,1024]{1,0:T(8,128)(2,1)S(1)} %bitcast.79), custom_call_target="tpu_custom_call" | custom-call | tf_op jit(solution)/shard_map/pallas_call | solution.py:297
  67.0 15.4 %shard_map.97 = bf16[4,128,1024]{2,1,0:T(8,128)(2,1)S(1)} custom-call(bf16[8,128,1024]{2,1,0:T(8,128)(2,1)S(1)} %bitcast.77), custom_call_target="tpu_custom_call" | custom-call | tf_op jit(solution)/shard_map/pallas_call | solution.py:109
  82.7 0.3 fusion.62
  83.1 2.4 %collective-permute-start.1 = (bf16[24,1024]{1,0:T(8,128)(2,1)S(1)}, bf16[24,1024]{1,0:T(8,128)(2,1)S(1)}, u32[]{:S(2)}, u32[]{:S(2)}) collective-permute-start(bf16[24,1024]{1,0:T(8,128)(2,1)S(1)} %get-tuple-element.42), channel_id=1, source_target_pairs={{0,4},{4,8},{8,12},{12,16},{16,20},{20,24},{24,28},{1,5},{5,9},{9,... | collective-permute-start | bytes 147464 | tf_op jit(solution)/shard_map/ppermute | solution.py:20
  85.4 1.3 %collective-permute-start = (bf16[24,1024]{1,0:T(8,128)(2,1)S(1)}, bf16[24,1024]{1,0:T(8,128)(2,1)S(1)}, u32[]{:S(2)}, u32[]{:S(2)}) collective-permute-start(bf16[24,1024]{1,0:T(8,128)(2,1)S(1)} %get-tuple-element.41), channel_id=1, source_target_pairs={{4,0},{8,4},{12,8},{16,12},{20,16},{24,20},{28,24},{5,1},{9,5},{13... | collective-permute-start | bytes 147464 | tf_op jit(solution)/shard_map/ppermute | solution.py:20
  86.7 0.8 fusion.13
  87.9 1.7 %collective-permute-done = bf16[24,1024]{1,0:T(8,128)(2,1)S(1)} collective-permute-done((bf16[24,1024]{1,0:T(8,128)(2,1)S(1)}, bf16[24,1024]{1,0:T(8,128)(2,1)S(1)}, u32[]{:S(2)}, u32[]{:S(2)}) %collective-permute-start) | collective-permute-done | bytes 49184 | tf_op jit(solution)/shard_map/ppermute | solution.py:20
  89.8 6.4 %shard_map.98 = bf16[4,32,1024]{2,1,0:T(8,128)(2,1)S(1)} custom-call(bf16[32,1024]{1,0:T(8,128)(2,1)S(1)} %pad.5.refs_0_), custom_call_target="tpu_custom_call" | custom-call | tf_op jit(solution)/shard_map/pallas_call | solution.py:203
  96.2 0.4 convolution_convert_fusion
  96.7 12.1 %shard_map.99 = bf16[8,96,256]{2,1,0:T(8,128)(2,1)S(1)} custom-call(bf16[96,256]{1,0:T(8,128)(2,1)S(1)} %bitcast.82), custom_call_target="tpu_custom_call" | custom-call | tf_op jit(solution)/shard_map/pallas_call | solution.py:203
  109.0 0.7 fusion.58
  109.8 0.3 select_reduce_fusion
  110.3 0.8 fusion.6
  (52 shorter events, 2.8 us)
Async XLA Ops:
  0.6 3.1 %copy-start = (bf16[512,1024]{1,0:T(8,128)(2,1)S(1)}, bf16[512,1024]{1,0:T(8,128)(2,1)}, u32[]{:S(2)}) copy-start(bf16[512,1024]{1,0:T(8,128)(2,1)} %param.14) | copy-start | bytes 3145732
  0.6 4.6 %slice-start = ((bf16[256,4352]{1,0:T(8,128)(2,1)}), bf16[256,256]{1,0:T(8,128)(2,1)S(1)}, s32[]{:S(2)}) async-start(bf16[256,4352]{1,0:T(8,128)(2,1)} %param.11), calls=%async_computation | async-start | bytes 262144 | tf_op jit(solution)/shard_map/slice | solution.py:334
  48.0 1.4 %copy-start.3 = (f32[4,2304]{1,0:T(4,128)S(1)}, f32[4,2304]{1,0:T(4,128)}, u32[]{:S(2)}) copy-start(f32[4,2304]{1,0:T(4,128)} %param.12) | copy-start | bytes 110596
  48.0 1.4 %slice-start.1 = ((f32[4,2304]{1,0:T(4,128)}), f32[4,256]{1,0:T(4,128)S(1)}, s32[]{:S(2)}) async-start(f32[4,2304]{1,0:T(4,128)} %param.12), calls=%async_computation.1 | async-start | bytes 8192 | tf_op jit(solution)/shard_map/slice | solution.py:376
  67.0 15.6 %copy-start.4 = (s32[1,192]{1,0:T(1,128)S(1)}, s32[1,192]{1,0:T(1,128)}, u32[]{:S(2)}) copy-start(s32[1,192]{1,0:T(1,128)} %param.10) | copy-start | bytes 2308
  67.0 15.7 %copy-start.1 = (bf16[1,128,1024]{2,1,0:T(8,128)(2,1)S(1)}, bf16[1,128,1024]{2,1,0:T(8,128)(2,1)}, u32[]{:S(2)}) copy-start(bf16[1,128,1024]{2,1,0:T(8,128)(2,1)} %param.8) | copy-start | bytes 786436
  82.4 5.2 %copy-start.2 = (bf16[1024,3,1,128]{3,0,2,1:T(8,128)(2,1)S(1)}, bf16[1024,3,1,128]{3,0,2,1:T(8,128)(2,1)}, u32[]{:S(2)}) copy-start(bf16[1024,3,1,128]{3,0,2,1:T(8,128)(2,1)} %param.15) | copy-start | bytes 2359300
  83.1 4.8 %collective-permute-start.1 = (bf16[24,1024]{1,0:T(8,128)(2,1)S(1)}, bf16[24,1024]{1,0:T(8,128)(2,1)S(1)}, u32[]{:S(2)}, u32[]{:S(2)}) collective-permute-start(bf16[24,1024]{1,0:T(8,128)(2,1)S(1)} %get-tuple-element.42), channel_id=1, source_target_pairs={{0,4},{4,8},{8,12},{12,16},{16,20},{20,24},{24,28},{1,5},{5,9},{9,... | collective-permute-start | bytes 147464 | tf_op jit(solution)/shard_map/ppermute | solution.py:20
  85.4 4.1 %collective-permute-start = (bf16[24,1024]{1,0:T(8,128)(2,1)S(1)}, bf16[24,1024]{1,0:T(8,128)(2,1)S(1)}, u32[]{:S(2)}, u32[]{:S(2)}) collective-permute-start(bf16[24,1024]{1,0:T(8,128)(2,1)S(1)} %get-tuple-element.41), channel_id=1, source_target_pairs={{4,0},{8,4},{12,8},{16,12},{20,16},{24,20},{28,24},{5,1},{9,5},{13... | collective-permute-start | bytes 147464 | tf_op jit(solution)/shard_map/ppermute | solution.py:20

commit v6 on v5

--- a/solution.py
+++ b/solution.py
@@ -233,7 +233,7 @@
 
 def mix_kernel(heads, convolved, gate, down, across, gain, back, share, state):
     length = convolved.shape[0]
-    width = gate.shape[1]
+    width = gain.shape[1]
     head_dim = width // heads
     state_width = (convolved.shape[1] - width) // 2
 
@@ -279,7 +279,7 @@
 
 def mix(convolved, gate, decays, gain, back):
     length, heads = decays.shape
-    blocks, width, model_width = length // BLOCK, gate.shape[1], back.shape[1]
+    blocks, width, model_width = length // BLOCK, gain.shape[1], back.shape[1]
     state_width = (convolved.shape[1] - width) // 2
     row = lax.broadcasted_iota(jnp.int32, (BLOCK, BLOCK), 0)
     column = lax.broadcasted_iota(jnp.int32, (BLOCK, BLOCK), 1)
@@ -300,7 +300,7 @@
         out_shape=jax.ShapeDtypeStruct((length, model_width), jnp.bfloat16),
         in_specs=[
             rows(convolved.shape[1]),
-            rows(width),
+            rows(gate.shape[1]),
             rows(heads),
             pl.BlockSpec((1, heads, BLOCK), lambda i: (i, 0, 0)),
             pl.BlockSpec((1, width), lambda i: (0, 0)),
@@ -382,7 +382,7 @@
     )
     convolved = convolve(padded, taps, length)
     gain = head_columns(norm_gain, 0, own_heads, head_dim, 0).reshape(1, width)
-    share = mix(convolved, projected[:, :width], own_decays, gain, back)
+    share = mix(convolved, projected, own_decays, gain, back)
     shares = pair_sums(1, share.reshape(seq_count, row_count, model_width))
     branch = jnp.sum(shares.astype(jnp.float32), axis=0)
     return (float_states + branch).astype(jnp.bfloat16)

time: 111 us -> 111 us (level)
  no operation moved by 1% of the time
where the time goes in v6:
time: 111 us
  Pallas kernels  84.6 us (76%)
  local copies, waits for them, and re-layouts  8.52 us (8%)
  other arithmetic  7.96 us (7%)
  matrix products  3.74 us (3%)
  starting transfers between devices  3.65 us (3%)
  waiting for transfers between devices  1.67 us (2%)
    pallas_call x3, Pallas kernels, exchange(): pl.pallas_call(functools.partial(exchange_kernel, plan), out_shape=shapes...  59.3 us
    pallas_call x1, Pallas kernels, pair_sums(): pl.pallas_call(pair_sum_kernel, out_shape=jax.ShapeDtypeStruct(block, sha...  15.4 us
    pallas_call x1, Pallas kernels, mix(): pl.pallas_call(functools.partial(mix_kernel, heads), grid=(blocks,), out_...  9.93 us
    dynamic_slice x6, local copies, waits for them, and re-layouts, head_columns(): lax.dynamic_slice_in_dim(array, first + head * head_dim, head_dim, axis)  4.34 us
    convert_element_type x1, other arithmetic, convolve(): return jax.nn.silu(summed).astype(jnp.bfloat16)  4.06 us
    ppermute x2, starting transfers between devices, passed_along(): lax.ppermute(value, axis, [(source, source + steps) for source in range(f...  3.65 us
  transfers between devices with their start and end apart: 2, of which 1 were waited for; matrix products, arithmetic and copies ran while one was open for 1% of the time, Pallas kernels for 0%

profile of v6, /device:TPU:0, one launch (start us, length us, event | category | flops | bytes accessed | tf_op | source)
XLA Modules:
  0.0 111.1 jit_solution(6159360666485079132)
XLA Ops:
  0.7 1.2 %fusion.10 = f32[128]{0:T(128)S(1)} fusion(bf16[1,128,1024]{2,1,0:T(8,128)(2,1)} %param.8), kind=kLoop, calls=%fused_computation.16 | loop fusion | flops 393088 | bytes 262656 | tf_op jit(solution)/shard_map/reduce_sum | solution.py:350
  1.9 1.1 fusion.11
  2.9 0.8 copy.39
  3.9 1.3 %constant_dynamic-slice_fusion.1 = (bf16[256,64]{1,0:T(8,128)(2,1)S(1)}, bf16[256,64]{1,0:T(8,128)(2,1)S(1)}, bf16[256,64]{1,0:T(8,128)(2,1)S(1)}, bf16[256,64]{...) fusion(bf16[256,4352]{1,0:T(8,128)(2,1)} %param.11, ...), kind=kLoop, calls=%fused_computation.86 | loop fusion | bytes 524320 | tf_op jit(solution)/shard_map/dynamic_slice | solution.py:227
  5.5 40.7 %shard_map.95 = (bf16[4,256,768]{2,1,0:T(8,128)(2,1)S(1)}, bf16[4,64,1024]{2,1,0:T(8,128)(2,1)S(1)}, bf16[8,128,1152]{2,1,0:T(8,128)(2,1)S(1)}) custom-call(bf16[256,768]{1,0:T(8,128)(2,1)S(1)} %concatenate.52.refs_0_, bf16[64,1024]{1,0:T(8,128)(2,1)S(1)} %constant_dynamic-slice_fusion.refs_1_, bf16[128,1152]{1,0:T(8,128)(2,1)S(1)} %concatenate.53.refs_2_), custom_call_target="tpu_custom_call" | custom-call | tf_op jit(solution)/shard_map/pallas_call | solution.py:203
  46.4 1.8 %fusion.2.gate = bf16[1024,768]{1,0:T(8,128)(2,1)S(1)} fusion(bf16[1024,768]{1,0:T(8,128)(2,1)S(1)} %bitcast.84, bf16[1024,1152]{1,0:T(8,128)(2,1)S(1)} %bitcast.81), kind=kOutput, calls=%fused_computation.4 | convolution fusion | flops 1611399168 | bytes 5242880 | tf_op jit(solution)/shard_map/dot_general | solution.py:360
  48.3 1.1 slice.94
  49.5 0.7 dynamic-slice_reduce_fusion.11
  50.3 1.3 %dynamic-slice_reduce_fusion.3 = (bf16[1024]{0:T(1024)(128)(2,1)S(1)}, bf16[1024]{0:T(1024)(128)(2,1)S(1)}, bf16[1024]{0:T(1024)(128)(2,1)S(1)}, bf16[1024]{0:T(...) fusion(bf16[1024,32]{1,0:T(8,128)(2,1)S(1)} %get-tuple-element., ...), kind=kLoop, calls=%fused_computation.24 | loop fusion | bytes 32784 | tf_op jit(solution)/shard_map/dynamic_slice | solution.py:227
  52.0 0.9 fusion.60
  53.0 4.1 %multiply_convert_fusion.convolved = bf16[1024,512]{1,0:T(8,128)(2,1)S(1)} fusion(bf16[1024,512]{1,0:T(8,128)(2,1)} %slice.94, f32[512]{0:T(512)S(1)} %bitcast.93, f32[512]{0:T(512)S(1)} %bitcast.94, f32[512]{0:T(512)S(1)} %bitcast.95, f32[512]{0:T(512)S(1)} %bitcast.92), kind=kLoop, calls=%fused_computation.3 | loop fusion | flops 8388608 | bytes 2105344 | tf_op jit(solution)/shard_map/convert_element_type | solution.py:27
  57.1 9.9 %shard_map.96 = bf16[1024,1024]{1,0:T(8,128)(2,1)S(1)} custom-call(bf16[1024,512]{1,0:T(8,128)(2,1)S(1)} %multiply_convert_fusion.convolved, bf16[1024,768]{1,0:T(8,128)(2,1)S(1)} %fusion.2.gate, f32[1024,4]{1,0:T(8,128)S(1)} %bitcast.78, f32[8,4,128]{2,1,0:T(4,128)S(1)} %copy.44.across, f32[1,256]{1,0:T(1,128)S(1)} %bitcast.83, bf16[256,1024]{1,0:T(8,128)(2,1)S(1)} %bitcast.79), custom_call_target="tpu_custom_call" | custom-call | tf_op jit(solution)/shard_map/pallas_call | solution.py:297
  67.0 15.4 %shard_map.97 = bf16[4,128,1024]{2,1,0:T(8,128)(2,1)S(1)} custom-call(bf16[8,128,1024]{2,1,0:T(8,128)(2,1)S(1)} %bitcast.77), custom_call_target="tpu_custom_call" | custom-call | tf_op jit(solution)/shard_map/pallas_call | solution.py:109
  82.8 0.3 fusion.62
  83.1 2.4 %collective-permute-start.1 = (bf16[24,1024]{1,0:T(8,128)(2,1)S(1)}, bf16[24,1024]{1,0:T(8,128)(2,1)S(1)}, u32[]{:S(2)}, u32[]{:S(2)}) collective-permute-start(bf16[24,1024]{1,0:T(8,128)(2,1)S(1)} %get-tuple-element.42), channel_id=1, source_target_pairs={{0,4},{4,8},{8,12},{12,16},{16,20},{20,24},{24,28},{1,5},{5,9},{9,... | collective-permute-start | bytes 147464 | tf_op jit(solution)/shard_map/ppermute | solution.py:20
  85.4 1.3 %collective-permute-start = (bf16[24,1024]{1,0:T(8,128)(2,1)S(1)}, bf16[24,1024]{1,0:T(8,128)(2,1)S(1)}, u32[]{:S(2)}, u32[]{:S(2)}) collective-permute-start(bf16[24,1024]{1,0:T(8,128)(2,1)S(1)} %get-tuple-element.41), channel_id=1, source_target_pairs={{4,0},{8,4},{12,8},{16,12},{20,16},{24,20},{28,24},{5,1},{9,5},{13... | collective-permute-start | bytes 147464 | tf_op jit(solution)/shard_map/ppermute | solution.py:20
  86.7 0.8 fusion.13
  87.9 1.7 %collective-permute-done = bf16[24,1024]{1,0:T(8,128)(2,1)S(1)} collective-permute-done((bf16[24,1024]{1,0:T(8,128)(2,1)S(1)}, bf16[24,1024]{1,0:T(8,128)(2,1)S(1)}, u32[]{:S(2)}, u32[]{:S(2)}) %collective-permute-start) | collective-permute-done | bytes 49184 | tf_op jit(solution)/shard_map/ppermute | solution.py:20
  89.8 6.4 %shard_map.98 = bf16[4,32,1024]{2,1,0:T(8,128)(2,1)S(1)} custom-call(bf16[32,1024]{1,0:T(8,128)(2,1)S(1)} %pad.5.refs_0_), custom_call_target="tpu_custom_call" | custom-call | tf_op jit(solution)/shard_map/pallas_call | solution.py:203
  96.2 0.4 convolution_convert_fusion
  96.7 12.2 %shard_map.99 = bf16[8,96,256]{2,1,0:T(8,128)(2,1)S(1)} custom-call(bf16[96,256]{1,0:T(8,128)(2,1)S(1)} %bitcast.82), custom_call_target="tpu_custom_call" | custom-call | tf_op jit(solution)/shard_map/pallas_call | solution.py:203
  109.0 0.7 fusion.58
  109.8 0.3 select_reduce_fusion
  110.3 0.8 fusion.6
  (55 shorter events, 2.7 us)
Async XLA Ops:
  0.6 3.1 %copy-start = (bf16[512,1024]{1,0:T(8,128)(2,1)S(1)}, bf16[512,1024]{1,0:T(8,128)(2,1)}, u32[]{:S(2)}) copy-start(bf16[512,1024]{1,0:T(8,128)(2,1)} %param.14) | copy-start | bytes 3145732
  0.6 4.6 %slice-start = ((bf16[256,4352]{1,0:T(8,128)(2,1)}), bf16[256,256]{1,0:T(8,128)(2,1)S(1)}, s32[]{:S(2)}) async-start(bf16[256,4352]{1,0:T(8,128)(2,1)} %param.11), calls=%async_computation | async-start | bytes 262144 | tf_op jit(solution)/shard_map/slice | solution.py:334
  46.2 2.0 %copy-start.1 = (bf16[4,64,1024]{2,1,0:T(8,128)(2,1)}, bf16[4,64,1024]{2,1,0:T(8,128)(2,1)S(1)}, u32[]{:S(2)}) copy-start(bf16[4,64,1024]{2,1,0:T(8,128)(2,1)S(1)} %get-tuple-element.7) | copy-start | bytes 1572868
  48.3 1.1 copy-start.5
  48.3 1.2 %slice-start.1 = ((f32[4,2304]{1,0:T(4,128)}), f32[4,256]{1,0:T(4,128)S(1)}, s32[]{:S(2)}) async-start(f32[4,2304]{1,0:T(4,128)} %param.12), calls=%async_computation.1 | async-start | bytes 8192 | tf_op jit(solution)/shard_map/slice | solution.py:376
  52.0 5.0 %copy-start.2 = (bf16[4,64,1024]{2,1,0:T(8,128)(2,1)S(1)}, bf16[4,64,1024]{2,1,0:T(8,128)(2,1)}, u32[]{:S(2)}) copy-start(bf16[4,64,1024]{2,1,0:T(8,128)(2,1)} %copy-done.1) | copy-start | bytes 1572868
  67.0 15.6 %copy-start.6 = (s32[1,192]{1,0:T(1,128)S(1)}, s32[1,192]{1,0:T(1,128)}, u32[]{:S(2)}) copy-start(s32[1,192]{1,0:T(1,128)} %param.10) | copy-start | bytes 2308
  67.0 15.7 %copy-start.3 = (bf16[1,128,1024]{2,1,0:T(8,128)(2,1)S(1)}, bf16[1,128,1024]{2,1,0:T(8,128)(2,1)}, u32[]{:S(2)}) copy-start(bf16[1,128,1024]{2,1,0:T(8,128)(2,1)} %param.8) | copy-start | bytes 786436
  82.4 5.2 %copy-start.4 = (bf16[1024,3,1,128]{3,0,2,1:T(8,128)(2,1)S(1)}, bf16[1024,3,1,128]{3,0,2,1:T(8,128)(2,1)}, u32[]{:S(2)}) copy-start(bf16[1024,3,1,128]{3,0,2,1:T(8,128)(2,1)} %param.15) | copy-start | bytes 2359300
  83.1 4.8 %collective-permute-start.1 = (bf16[24,1024]{1,0:T(8,128)(2,1)S(1)}, bf16[24,1024]{1,0:T(8,128)(2,1)S(1)}, u32[]{:S(2)}, u32[]{:S(2)}) collective-permute-start(bf16[24,1024]{1,0:T(8,128)(2,1)S(1)} %get-tuple-element.42), channel_id=1, source_target_pairs={{0,4},{4,8},{8,12},{12,16},{16,20},{20,24},{24,28},{1,5},{5,9},{9,... | collective-permute-start | bytes 147464 | tf_op jit(solution)/shard_map/ppermute | solution.py:20
  85.4 4.1 %collective-permute-start = (bf16[24,1024]{1,0:T(8,128)(2,1)S(1)}, bf16[24,1024]{1,0:T(8,128)(2,1)S(1)}, u32[]{:S(2)}, u32[]{:S(2)}) collective-permute-start(bf16[24,1024]{1,0:T(8,128)(2,1)S(1)} %get-tuple-element.41), channel_id=1, source_target_pairs={{4,0},{8,4},{12,8},{16,12},{20,16},{24,20},{28,24},{5,1},{9,5},{13... | collective-permute-start | bytes 147464 | tf_op jit(solution)/shard_map/ppermute | solution.py:20
